TPU v7x, 32 devices: a whole 2x2x4 slice. The times are simulated.
32 devices in a mesh: lang: 4 (over x, core), blk: 8 (over z, y).
Axes of the slice: x: 2, y: 2, z: 4, core: 2. Of those that a mesh axis runs over, the one named last changes fastest.
Arguments:
- fisher: bfloat16 [8, 4096, 16384], P('lang', None, 'blk'), may hold values from 0.049804688 to 5
- factor_left: bfloat16 [8, 4096, 64], P('lang', 'blk'), may hold values from -6 to 6
- factor_right: bfloat16 [8, 64, 16384], P('lang', None, 'blk'), may hold values from -0.75 to 0.75
- base_weight: bfloat16 [4096, 16384], P(('lang', 'blk')), may hold values from -3 to 3
Outputs:
- merged: bfloat16 [4096, 16384], P(('lang', 'blk'))
All inputs are finite; a program needn't handle non-finite values.
Results may differ from a plain program's by a relative error of at most 0.0011.
Values may be sent and summed in bfloat16 or wider, within the bound.
No kernel may reach another device: no remote copies, remote signals or barrier semaphores. Data moves between devices by JAX's collectives and lax.ppermute only.
A program may use at most 256 MiB of HBM per device.

v0:
```python
import jax
import jax.numpy as jnp
from jax import lax
from jax.sharding import PartitionSpec as P


def weighted_sums(fisher_part, change):
    weight_wide = fisher_part.astype(jnp.float32)
    return (jnp.sum(weight_wide * change, axis=0), jnp.sum(weight_wide, axis=0))


def shards(fisher, factor_left, factor_right, base_weight):
    lang_count = lax.axis_size("lang")
    blk_count = lax.axis_size("blk")
    local_langs, full_rows, columns = fisher.shape
    row_count = base_weight.shape[0]
    change = jnp.einsum(
        "lir,lrc->lic",
        lax.all_gather(factor_left, "blk", axis=1, tiled=True),
        factor_right,
        preferred_element_type=jnp.float32,
    )
    weighted, totals = weighted_sums(fisher, change)
    weighted = weighted.reshape(lang_count, blk_count, row_count, columns)
    totals = totals.reshape(lang_count, blk_count, row_count, columns)
    moved = (
        lax.all_to_all(weighted, "blk", split_axis=1, concat_axis=3, tiled=True),
        lax.all_to_all(totals, "blk", split_axis=1, concat_axis=3, tiled=True),
    )
    weighted, totals = (
        lax.psum_scatter(moved[0], "lang", scatter_dimension=0, tiled=True),
        lax.psum_scatter(moved[1], "lang", scatter_dimension=0, tiled=True),
    )
    weighted = weighted.reshape(row_count, columns * blk_count)
    totals = totals.reshape(row_count, columns * blk_count)
    return (base_weight.astype(jnp.float32) + weighted / totals).astype(jnp.bfloat16)


def solution(mesh):
    placed = (
        P("lang", None, "blk"),
        P("lang", "blk", None),
        P("lang", None, "blk"),
        P(("lang", "blk"), None),
    )
    return jax.shard_map(
        shards, mesh=mesh, in_specs=placed, out_specs=P(("lang", "blk"), None), check_vma=False
    )
```

profile of v0, /device:TPU:0, one launch (start us, length us, event | category | flops | bytes accessed | tf_op | source)
XLA Modules:
  0.0 1913.3 jit_solution(13532211394570988480)
XLA Ops:
  7.4 0.0 copy-start
  7.4 31.8 %convert_reduce_fusion = f32[4096,2048]{1,0:T(8,128)} fusion(bf16[2,4096,2048]{2,1,0:T(8,128)(2,1)} %param.4), kind=kLoop, calls=%fused_computation | loop fusion | flops 25165824 | bytes 67108864 | tf_op jit(solution)/shard_map/reduce_sum | solution.py:9
  39.2 23.0 %copy.12 = f32[4,8,128,2048]{3,2,0,1:T(8,128)} copy(f32[4,8,128,2048]{3,2,1,0:T(8,128)} %bitcast.21) | data formatting | bytes 67108864 | tf_op jit(solution)/shard_map/reshape | solution.py:25
  62.2 7.3 all-to-all-start.1
  69.5 0.0 all-gather.2.cloned.1.call-start
  69.6 0.7 all-gather.2.cloned.1.call-update
  70.2 0.0 reduce-scatter.5.cloned.1.call-start
  70.3 735.8 %all-to-all-done.1 = f32[4,8,128,2048]{3,2,0,1:T(8,128)} async-done(((f32[4,8,128,2048]{3,2,0,1:T(8,128)}), f32[4,8,128,2048]{3,2,0,1:T(8,128)}, u32[]{:S(2)}, u32[]{:S(2)}) %all-to-all-start.1) | async-done | bytes 33554464 | tf_op jit(solution)/shard_map/all_to_all | solution.py:28
  806.1 33.8 %copy.13 = f32[4,8,128,2048]{2,3,1,0:T(8,128)} copy(f32[4,8,128,2048]{3,2,0,1:T(8,128)} %all-to-all-done.1) | data formatting | bytes 67108864 | tf_op jit(solution)/shard_map/all_to_all | solution.py:28
  839.9 0.0 reduce-scatter.5.cloned.1.call-update
  839.9 0.0 reduce-scatter.3.cloned.1.call-start
  840.0 0.0 all-gather.2.cloned.1.call-done
  840.0 0.0 copy-done
  840.0 42.6 %fusion = f32[4096,2048]{1,0:T(8,128)} fusion(bf16[2,4096,2048]{2,1,0:T(8,128)(2,1)} %param.4, bf16[2,4096,64]{1,2,0:T(8,128)(2,1)} %all-gather.2.cloned.1.call-done, bf16[2,64,2048]{2,1,0:T(8,128)(2,1)S(1)} %copy-done), kind=kOutput, calls=%fused_computation.2 | convolution fusion | flops 2189426688 | bytes 68681728 | tf_op jit(solution)/shard_map/lir,lrc->lic/dot_general | solution.py:17
  882.6 12.7 copy.10
  895.3 728.3 %all_to_all.36 = f32[4,8,128,2048]{3,2,0,1:T(8,128)} all-to-all(f32[4,8,128,2048]{3,2,0,1:T(8,128)S(1)} %copy.10), channel_id=1, replica_groups=mesh['lang'=4,'blk'=8] {'blk'}, dimensions={1} | all-to-all | bytes 67108864 | tf_op jit(solution)/shard_map/all_to_all | solution.py:27
  1623.5 33.8 %copy.11 = f32[4,8,128,2048]{2,3,1,0:T(8,128)} copy(f32[4,8,128,2048]{3,2,0,1:T(8,128)} %all_to_all.36) | data formatting | bytes 67108864 | tf_op jit(solution)/shard_map/all_to_all | solution.py:27
  1657.4 0.0 copy-start.1
  1657.4 0.0 reduce-scatter.3.cloned.1.call-update
  1657.4 6.5 copy.9
  1663.9 225.8 %reduce-scatter.3.cloned.1.call-done = f32[1,1,128,16384]{2,3,0,1:T(8,128)} async-done(((f32[4,1,128,16384]{2,3,0,1:T(8,128)}), f32[1,1,128,16384]{2,3,0,1:T(8,128)}) %reduce-scatter.3.cloned.1.call-update) | async-done | bytes 8388624 | tf_op jit(solution)/shard_map/reduce_scatter | solution.py:31
  1889.7 9.8 fusion.1
  1899.5 6.4 copy.14
  1905.8 0.0 copy-done.1
  (1 shorter events, 0.0 us)
Async XLA Ops:
  7.4 832.6 %copy-start = (bf16[2,64,2048]{2,1,0:T(8,128)(2,1)S(1)}, bf16[2,64,2048]{2,1,0:T(8,128)(2,1)}, u32[]{:S(2)}) copy-start(bf16[2,64,2048]{2,1,0:T(8,128)(2,1)} %param.6) | copy-start | bytes 1572868
  62.2 743.8 %all-to-all-start.1 = ((f32[4,8,128,2048]{3,2,0,1:T(8,128)}), f32[4,8,128,2048]{3,2,0,1:T(8,128)}, u32[]{:S(2)}, u32[]{:S(2)}) async-start(f32[4,8,128,2048]{3,2,0,1:T(8,128)} %copy.12), calls=%async_computation.2 | async-start | bytes 67108864 | tf_op jit(solution)/shard_map/all_to_all | solution.py:28
  69.5 770.5 %all-gather.2.cloned.1.call-start = ((), (), s32[]{:S(2)}) async-start(), calls=%async_computation.4 | async-start | bytes 1179648 | tf_op jit(solution)/shard_map/all_gather | solution.py:19
  70.2 1593.7 %reduce-scatter.5.cloned.1.call-start = ((), (), s32[]{:S(2)}) async-start(), calls=%async_computation.6 | async-start | bytes 41943040 | tf_op jit(solution)/shard_map/reduce_scatter | solution.py:32
  839.9 1049.7 %reduce-scatter.3.cloned.1.call-start = ((), (), s32[]{:S(2)}) async-start(), calls=%async_computation.5 | async-start | bytes 41943040 | tf_op jit(solution)/shard_map/reduce_scatter | solution.py:31
  1657.4 248.5 %copy-start.1 = (bf16[2,64,2048]{2,1,0:T(8,128)(2,1)S(1)}, bf16[2,64,2048]{2,1,0:T(8,128)(2,1)}, u32[]{:S(2)}) copy-start(bf16[2,64,2048]{2,1,0:T(8,128)(2,1)} %param.6) | copy-start | bytes 1572868
Sparse Core Ops, SparseCore 0:
  72.4 560.9 all-gather.1
Sparse Core Ops, SparseCore 1:
  840.0 233.8 reduce-scatter.4
  1657.5 232.1 reduce-scatter.2
where the time goes:
time: 1920 us; the launch traced here: 1910 us
  waiting for transfers between devices  962 us (50%)
  blocking collectives  728 us (38%)
  local copies, waits for them, and re-layouts  116 us (6%)
  matrix products  42.6 us (2%)
  other arithmetic  41.7 us (2%)
    all_to_all x1, waiting for transfers between devices, shards(): lax.all_to_all(totals, 'blk', split_axis=1, concat_axis=3, tiled=True)  736 us
    all_to_all x1, blocking collectives, shards(): lax.all_to_all(weighted, 'blk', split_axis=1, concat_axis=3, tiled=True)  728 us
    reduce_scatter x1, waiting for transfers between devices, shards(): lax.psum_scatter(moved[0], 'lang', scatter_dimension=0, tiled=True)  226 us
    dot_general x1, matrix products, shards(): jnp.einsum('lir,lrc->lic', lax.all_gather(factor_left, 'blk', axis=1, til...  42.6 us
  transfers between devices with their start and end apart: 4, of which 2 were waited for; matrix products, arithmetic and copies ran while one was open for 7% of the time, Pallas kernels for 0%

commit v1 on v0

v1 whole, which is shorter than its diff:
```python
import functools

import jax
import jax.numpy as jnp
from jax import lax
from jax.experimental import pallas as pl
from jax.experimental.pallas import tpu as pltpu
from jax.sharding import PartitionSpec as P

F32 = jnp.float32
BF16 = jnp.bfloat16
TINY = 2.0**-126
LAG = 4
VMEM = 64 * 1024 * 1024 - 128 * 1024


def encode_total(t):
    t = t * 0.5
    for _ in range(5):
        t = t * t
    return t.astype(BF16)


def decode_total(code):
    t = code.astype(F32)
    for _ in range(4):
        t = lax.rsqrt(t)
    return 2.0 * t * lax.rsqrt(t)


def encode_signed(v):
    v2 = v * v
    v4 = v2 * v2
    return (v4 * v2 * (v * jnp.abs(v))).astype(BF16)


def decode_signed(code):
    code = code.astype(F32)
    a = lax.rsqrt(jnp.maximum(jnp.abs(code), TINY))
    d = lax.rsqrt(lax.rsqrt(a))
    return code * a * (d * d * d)


def sum_totals(fishers):
    total = None
    for ref in fishers:
        for lang in range(ref.shape[0]):
            wide = ref[lang].astype(F32)
            total = wide if total is None else total + wide
    return total


def sum_weighted(fishers, lefts, rights):
    weighted = None
    for ref, left, right in zip(fishers, lefts, rights):
        rank = right.shape[1]
        for lang in range(ref.shape[0]):
            change = jnp.dot(left[:, lang * rank : (lang + 1) * rank], right[lang], preferred_element_type=F32)
            term = ref[lang].astype(F32) * change
            weighted = term if weighted is None else weighted + term
    return weighted


def sum_all(fishers, lefts, rights):
    totals, weighted = None, None
    for ref, left, right in zip(fishers, lefts, rights):
        rank = right.shape[1]
        for lang in range(ref.shape[0]):
            change = jnp.dot(left[:, lang * rank : (lang + 1) * rank], right[lang], preferred_element_type=F32)
            wide = ref[lang].astype(F32)
            totals = wide if totals is None else totals + wide
            weighted = wide * change if weighted is None else weighted + wide * change
    return totals, weighted


def copy_body(src, out):
    out[...] = src[...]


def totals_body(own, peer, out):
    out[...] = encode_total(sum_totals((own, peer)))


def weighted_body(own, peer, left_own, left_peer, right_own, right_peer, out):
    _, weighted = sum_all((own, peer), (left_own, left_peer), (right_own, right_peer))
    out[...] = encode_signed(weighted)


def both_body(own, peer, left_own, left_peer, right_own, right_peer, out_totals, out_weighted):
    totals, weighted = sum_all((own, peer), (left_own, left_peer), (right_own, right_peer))
    out_totals[...] = encode_total(totals)
    out_weighted[...] = encode_signed(weighted)


def ratio(own, peer, left_own, left_peer, right_own, right_peer, total_code, weighted_code):
    totals, weighted = sum_all((own, peer), (left_own, left_peer), (right_own, right_peer))
    return (weighted + decode_signed(weighted_code[...])) / (totals + decode_total(total_code[...]))


def ratio_body(*refs):
    refs[-1][...] = encode_signed(ratio(*refs[:8]))


def merge_own_body(*refs):
    refs[-1][...] = (refs[8][...].astype(F32) + ratio(*refs[:8])).astype(BF16)


def merge_body(code, base, out):
    out[...] = (base[...].astype(F32) + decode_signed(code[...])).astype(BF16)


def merge_many_body(*refs):
    *codes, base, out = refs
    for i, code in enumerate(codes):

        @pl.when(pl.program_id(0) == i)
        def _():
            merge_body(code, base, out)


def run_parts(parts, skipped, place, *refs):
    taken = sum(count for _, count, _ in parts)
    ins, outs = refs[:taken], refs[taken + skipped :]
    for body, count, results in parts:
        body(*ins[:count], *outs[:results])
        ins, outs = ins[count:], outs[results:]


def shards(fisher, factor_left, factor_right, base_weight):
    lang_count = lax.axis_size("lang")
    blk_count = lax.axis_size("blk")
    langs, full_rows, cols = fisher.shape
    rows = base_weight.shape[0]
    rank = factor_right.shape[1]
    steps = 8
    group = blk_count // steps
    band = group * rows
    tile = min(1024, cols)
    tiles = cols // tile
    half = lang_count // 2
    sides = half

    lang, blk = lax.axis_index("lang"), lax.axis_index("blk")
    core, side = lax.rem(lang, 2), lax.div(lang, 2)
    high = lax.div(blk, group)

    def over_core(a):
        return lax.ppermute(a, "lang", [(i, i ^ 1) for i in range(lang_count)])

    def over_x(a):
        return lax.ppermute(a, "lang", [(i, i ^ half) for i in range(lang_count)])

    bands = fisher.reshape(langs, lang_count * steps, band, cols)
    by_owner = fisher.reshape(langs, sides, 2 * steps, band, cols)

    ANY = pl.BlockSpec(memory_space=pl.ANY)
    last = [None]

    def call(parts, deps=(), alias=None, grid=(tiles,)):
        counts = [(body, len(operands), len(shapes)) for body, operands, _, shapes, _ in parts]
        operands, specs, shapes, out_specs = ([one for part in parts for one in part[k]] for k in range(1, 5))
        deps = list(deps) + ([last[0]] if last[0] is not None and last[0] is not alias else [])
        tail = deps + ([alias] if alias is not None else [])
        results = pl.pallas_call(
            functools.partial(run_parts, counts, len(tail)),
            out_shape=shapes,
            grid_spec=pltpu.PrefetchScalarGridSpec(
                num_scalar_prefetch=1,
                grid=grid,
                in_specs=specs + [ANY] * len(tail),
                out_specs=out_specs,
            ),
            input_output_aliases={} if alias is None else {len(operands) + len(tail): 0},
            compiler_params=pltpu.CompilerParams(vmem_limit_bytes=VMEM),
        )(place, *operands, *tail)
        last[0] = results[0]
        return list(results)

    place = jnp.stack([high, core, side, blk]).astype(jnp.int32)

    def owner(s, far, step):
        at_side = 1 - s[2] if far else s[2]
        return (at_side * 2 + s[1]) * steps + lax.bitwise_xor(s[0], step)

    right_peer = over_core(factor_right)
    left = factor_left.transpose(1, 0, 2).reshape(-1, langs * rank)
    shard_rows = left.shape[0]
    rounds = []
    relative = shard_rows % band == 0
    if relative:
        bit = blk_count // 2
        while bit:
            left = jnp.concatenate([left, lax.ppermute(left, "blk", [(i, i ^ bit) for i in range(blk_count)])])
            rounds.append(left)
            bit //= 2
    else:
        left = lax.all_gather(left, "blk", axis=0, tiled=True)
    left_peer = over_core(left).reshape(-1, band, langs * rank)
    left_bands = left.reshape(-1, band, langs * rank)

    def left_band(s, far, step):
        index = owner(s, far, step)
        if not relative:
            return index
        inside = shard_rows // band
        apart = lax.bitwise_xor(lax.div(index, inside), s[3])
        shard, bit = 0, blk_count // 2
        while bit:
            shard, apart, bit = shard + lax.rem(apart, 2) * bit, lax.div(apart, 2), bit // 2
        return shard * inside + lax.rem(index, inside)

    factors = (left_bands, left_peer, factor_right, right_peer)

    code_shape = jax.ShapeDtypeStruct((band, cols), BF16)
    out_shape = jax.ShapeDtypeStruct(base_weight.shape, BF16)

    right_spec = pl.BlockSpec((langs, rank, tile), lambda j, s: (0, 0, j))
    flat_spec = pl.BlockSpec((band, tile), lambda j, s: (0, j))

    def fisher_specs(far, step, whole):
        own = pl.BlockSpec((langs, None, band, tile), lambda j, s: (0, owner(s, far, step), 0, j))
        if whole:
            return own, pl.BlockSpec((langs, None, band, tile), lambda j, s: (0, 1 - s[2] if far else s[2], 0, j))
        return own, pl.BlockSpec((langs, None, band, tile), lambda j, s: (0, 0, 0, j))

    def factor_specs(far, step):
        return (
            pl.BlockSpec((None, band, langs * rank), lambda j, s: (left_band(s, far, step), 0, 0)),
            pl.BlockSpec((None, band, langs * rank), lambda j, s: (left_band(s, far, step), 0, 0)),
            right_spec,
            right_spec,
        )

    order = [7, 6, 5, 4, 3, 2, 1, 0]
    peers = {}
    arrived = {}
    crossed = []
    ratios = {}

    def copy_part(step, far=None):
        def other(s):
            return (1 - s[1]) * steps + lax.bitwise_xor(s[0], step)

        if far is None:
            src = pl.BlockSpec((langs, sides, None, band, tile), lambda j, s: (0, 0, other(s), 0, j))
            out = pl.BlockSpec((langs, sides, band, tile), lambda j, s: (0, 0, 0, j))
            shape = jax.ShapeDtypeStruct((langs, sides, band, cols), BF16)
        else:
            src = pl.BlockSpec((langs, 1, None, band, tile), lambda j, s: (0, 1 - s[2] if far else s[2], other(s), 0, j))
            out = pl.BlockSpec((langs, 1, band, tile), lambda j, s: (0, 0, 0, j))
            shape = jax.ShapeDtypeStruct((langs, 1, band, cols), BF16)
        return copy_body, (by_owner,), (src,), [shape], [out]

    def exchange(where, piece):
        step, far = (*where, None)[:2]
        piece = over_core(piece)
        for which in (True, False) if far is None else (far,):
            peers[step, which] = (piece, far is None)

    def send_part(body, step):
        peer, whole = peers[step, True]
        operands, specs = (bands, peer), fisher_specs(True, step, whole)
        if body is not totals_body:
            operands, specs = operands + factors, specs + factor_specs(True, step)
        codes = 2 if body is both_body else 1
        return body, operands, specs, [code_shape] * codes, [flat_spec] * codes

    def near_operands(step):
        peer, whole = peers[step, False]
        return (bands, peer, *factors, *arrived[step]), (*fisher_specs(False, step, whole), *factor_specs(False, step), flat_spec, flat_spec)

    def divide_part(step):
        return ratio_body, *near_operands(step), [code_shape], [flat_spec]

    def to_owner(step, code):
        if step:
            code = lax.ppermute(code, "blk", [(i, i ^ (step * group)) for i in range(blk_count)])
        if group > 1:
            near_groups = [[h * group + g for g in range(group)] for h in range(steps)]
            code = lax.all_to_all(code.reshape(group, rows, cols), "blk", 0, 0, axis_index_groups=near_groups, tiled=True)
        ratios[step] = code.reshape(group, rows, cols)

    def stage(send=None, copies=(), divide=None, deps=()):
        parts = []
        if send is not None:
            parts.append(send_part(*send))
        for copy in copies:
            parts.append(copy_part(*copy))
        if divide is not None:
            parts.append(divide_part(divide))
        late = list(ratios.values())[-LAG:][:1] if len(ratios) >= LAG else []
        results = call(parts, deps=list(deps) + (crossed[-2] if len(crossed) > 1 else []) + late)
        if send is not None:
            body, step = send
            codes, results = results[: len(parts[0][3])], results[len(parts[0][3]) :]
            crossed.append([over_x(code) for code in codes])
            arrived.setdefault(step, []).extend(crossed[-1])
        for copy in copies:
            exchange(copy, results.pop(0))
        if divide is not None:
            to_owner(divide, results.pop(0))

    a = order
    stage(copies=[(a[0], True)])
    stage(copies=[(a[1],), (a[2],)])
    stage((totals_body, a[0]), copies=[(a[3],), (a[0], False)], deps=rounds[:1])
    stage((totals_body, a[1]), copies=[(a[4],)])
    stage((totals_body, a[2]), copies=[(a[5],)], deps=rounds[1:2])
    stage((totals_body, a[3]), copies=[(a[6],)])
    stage((totals_body, a[4]), copies=[(a[7],)], deps=rounds[2:])
    stage((weighted_body, a[0]))
    stage((weighted_body, a[1]))
    stage((weighted_body, a[2]), divide=a[0])
    stage((weighted_body, a[3]), divide=a[1])
    stage((weighted_body, a[4]), divide=a[2])
    stage((both_body, a[5]), divide=a[3])
    stage((both_body, a[6]), divide=a[4])
    stage((both_body, a[7]), divide=a[5])
    stage(divide=a[6])
    merged = None

    def merge(done):
        nonlocal merged
        for part in range(group):

            def column(i, s, part=part):
                step = done[0]
                for n in range(1, len(done)):
                    step = jnp.where(i == n, done[n], step)
                return (0, lax.bitwise_xor(s[0], step) * group + part)

            code_spec = pl.BlockSpec((None, rows, cols), lambda i, s, part=part: (part, 0, 0))
            column_spec = pl.BlockSpec((rows, cols), column)
            merged = call(
                [(merge_many_body, (*(ratios[step] for step in done), base_weight), (code_spec,) * len(done) + (column_spec,), [out_shape], [column_spec])],
                alias=merged,
                grid=(len(done),),
            )[0]

    merge(a[:4])
    merge(a[4:6])
    if group == 1:
        merge(a[6:7])
        operands, specs = near_operands(a[7])
        column_spec = pl.BlockSpec((rows, tile), lambda j, s: (0, lax.bitwise_xor(s[0], a[7]) * tiles + j))
        merged = call([(merge_own_body, (*operands, base_weight), (*specs, column_spec), [out_shape], [column_spec])], alias=merged)[0]
    else:
        stage(divide=a[7])
        merge(a[6:])
    return merged


def solution(mesh):
    placed = (
        P("lang", None, "blk"),
        P("lang", "blk", None),
        P("lang", None, "blk"),
        P(("lang", "blk"), None),
    )
    return jax.shard_map(
        shards, mesh=mesh, in_specs=placed, out_specs=P(("lang", "blk"), None), check_vma=False
    )
```

time: 1920 us -> 254 us (0.13)
  waiting for transfers between devices: 962 us -> 76.5 us
  blocking collectives: 728 us -> 0 us
  local copies, waits for them, and re-layouts: 116 us -> 1.83 us
  Pallas kernels: 0 us -> 101 us
  starting transfers between devices: 7.4 us -> 69.1 us
  matrix products: 42.6 us -> 0 us
  other arithmetic: 41.7 us -> 4.44 us
    all_to_all x1 -> x0, waiting for transfers between devices: 736 us -> none  [shards(): lax.all_to_all(totals, 'blk', split_axis=1, concat_axis=3, tiled=True)]
    all_to_all x1 -> x0, blocking collectives: 728 us -> none  [shards(): lax.all_to_all(weighted, 'blk', split_axis=1, concat_axis=3, tiled=True)]
    reduce_scatter x2 -> x0, waiting for transfers between devices: 226 us -> none  [the longest x1 226 us: shards(): lax.psum_scatter(moved[0], 'lang', scatter_dimension=0, tiled=True)]
    pallas_call x0 -> x20, Pallas kernels: none -> 101 us  [call(): pl.pallas_call(functools.partial(run_parts, counts, len(tail)), out_shape...]
    ppermute x0 -> x37, waiting for transfers between devices: none -> 76.5 us  [the longest x16 33.6 us: over_x(): return lax.ppermute(a, 'lang', [(i, i ^ half) for i in range(lang_count)])]
    ppermute x0 -> x37, starting transfers between devices: none -> 69.1 us  [the longest x7 39.1 us: to_owner(): lax.ppermute(code, 'blk', [(i, i ^ step * group) for i in range(blk_count)])]
    all_to_all x2 -> x0, local copies, waits for them, and re-layouts: 67.7 us -> none  [the longest x1 33.8 us: shards(): lax.all_to_all(weighted, 'blk', split_axis=1, concat_axis=3, tiled=True)]
    dot_general x1 -> x0, matrix products: 42.6 us -> none  [shards(): jnp.einsum('lir,lrc->lic', lax.all_gather(factor_left, 'blk', axis=1, til...]
  transfers between devices with their start and end apart: 4 -> 37, of which waited for: 2 -> 14; matrix products, arithmetic and copies ran while one was open for 7% -> 2% of each run, Pallas kernels for 0% -> 35%
where the time goes in v1:
time: 254 us; the launch traced here: 253 us
  Pallas kernels  101 us (40%)
  waiting for transfers between devices  76.5 us (30%)
  starting transfers between devices  69.1 us (27%)
  other arithmetic  4.44 us (2%)
    pallas_call x20, Pallas kernels, call(): pl.pallas_call(functools.partial(run_parts, counts, len(tail)), out_shape...  101 us
    ppermute x7, starting transfers between devices, to_owner(): lax.ppermute(code, 'blk', [(i, i ^ step * group) for i in range(blk_count)])  39.1 us
    ppermute x16, waiting for transfers between devices, over_x(): return lax.ppermute(a, 'lang', [(i, i ^ half) for i in range(lang_count)])  33.6 us
    ppermute x3, waiting for transfers between devices, shards(): lax.ppermute(left, 'blk', [(i, i ^ bit) for i in range(blk_count)])  24.4 us
    ppermute x16, starting transfers between devices, over_x(): return lax.ppermute(a, 'lang', [(i, i ^ half) for i in range(lang_count)])  21.2 us
    ppermute x7, waiting for transfers between devices, to_owner(): lax.ppermute(code, 'blk', [(i, i ^ step * group) for i in range(blk_count)])  18.4 us
    ppermute x3, starting transfers between devices, shards(): lax.ppermute(left, 'blk', [(i, i ^ bit) for i in range(blk_count)])  6.26 us
  transfers between devices with their start and end apart: 37, of which 14 were waited for; matrix products, arithmetic and copies ran while one was open for 2% of the time, Pallas kernels for 35%

profile of v1, /device:TPU:0, one launch (start us, length us, event | category | flops | bytes accessed | tf_op | source)
XLA Modules:
  0.0 253.4 jit_solution(4206704901986760876)
XLA Ops:
  3.4 4.4 %shard_map.47 = (bf16[2,2,128,2048]{3,2,1,0:T(8,128)(2,1)}, bf16[2,2,128,2048]{3,2,1,0:T(8,128)(2,1)}) custom-call(s32[4]{0:T(128)} %pad_add_fusion.place, bf16[2,2,16,128,2048]{4,3,2,1,0:T(8,128)(2,1)} %bitcast.18, bf16[2,2,16,128,2048]{4,3,2,1,0:T(8,128)(2,1)} %bitcast.19, bf16[2,1,128,2048]{3,2,1,0:T(8,128)(2,1)} %shard_map.46.refs_2_), custom_call_target="tpu_custom_call" | custom-call | tf_op jit(solution)/shard_map/pallas_call | solution.py:164
  13.5 7.0 %collective-permute-done.2 = bf16[512,128]{1,0:T(8,128)(2,1)S(1)} collective-permute-done((bf16[512,128]{1,0:T(8,128)(2,1)S(1)}, bf16[512,128]{1,0:T(8,128)(2,1)S(1)}, u32[]{:S(2)}, u32[]{:S(2)}) %collective-permute-start.2) | collective-permute-done | bytes 131104 | tf_op jit(solution)/shard_map/ppermute | solution.py:193
  21.2 4.5 %shard_map.48 = (bf16[128,2048]{1,0:T(8,128)(2,1)}, bf16[2,2,128,2048]{3,2,1,0:T(8,128)(2,1)}, bf16[2,1,128,2048]{3,2,1,0:T(8,128)(2,1)}) custom-call(s32[4]{0:T(128)} %pad_add_fusion.place, bf16[2,32,128,2048]{3,2,1,0:T(8,128)(2,1)} %bitcast.20, bf16[2,1,128,2048]{3,2,1,0:T(8,128)(2,1)} %collective-permute-done.1.refs_1_, ...), custom_call_target="tpu_custom_call" | custom-call | tf_op jit(solution)/shard_map/pallas_call | solution.py:164
  31.5 7.5 %collective-permute-done.4 = bf16[1024,128]{1,0:T(8,128)(2,1)S(1)} collective-permute-done((bf16[1024,128]{1,0:T(8,128)(2,1)}, bf16[1024,128]{1,0:T(8,128)(2,1)S(1)}, u32[]{:S(2)}, u32[]{:S(2)}) %collective-permute-start.4) | collective-permute-done | bytes 262176 | tf_op jit(solution)/shard_map/ppermute | solution.py:193
  43.9 10.0 %collective-permute-done.5 = bf16[2048,128]{1,0:T(8,128)(2,1)S(1)} collective-permute-done((bf16[2048,128]{1,0:T(8,128)(2,1)S(1)}, bf16[2048,128]{1,0:T(8,128)(2,1)S(1)}, u32[]{:S(2)}, u32[]{:S(2)}) %collective-permute-start.5) | collective-permute-done | bytes 524320 | tf_op jit(solution)/shard_map/ppermute | solution.py:193
  57.9 4.3 %shard_map.50 = (bf16[128,2048]{1,0:T(8,128)(2,1)}, bf16[2,2,128,2048]{3,2,1,0:T(8,128)(2,1)}) custom-call(s32[4]{0:T(128)} %pad_add_fusion.place, bf16[2,32,128,2048]{3,2,1,0:T(8,128)(2,1)} %bitcast.25, bf16[2,2,128,2048]{3,2,1,0:T(8,128)(2,1)} %collective-permute-done.6.refs_1_.refs_7_, bf16[2,2,16,128,2048]{4,3,2,1,0:T(8,128)(2,1)} %bitcast.26, ...), custom_call_target="tpu_custom_call" | custom-call | tf_op jit(solution)/shard_map/pallas_call | solution.py:164
  62.2 4.5 %collective-permute-done.10.refs_3_.refs_12_ = bf16[128,2048]{1,0:T(8,128)(2,1)} collective-permute-done((bf16[128,2048]{1,0:T(8,128)(2,1)}, bf16[128,2048]{1,0:T(8,128)(2,1)}, u32[]{:S(2)}, u32[]{:S(2)}) %collective-permute-start.10) | collective-permute-done | bytes 524320 | tf_op jit(solution)/shard_map/ppermute | solution.py:151
  68.2 4.2 %shard_map.51 = (bf16[128,2048]{1,0:T(8,128)(2,1)}, bf16[2,2,128,2048]{3,2,1,0:T(8,128)(2,1)}) custom-call(s32[4]{0:T(128)} %pad_add_fusion.place, bf16[2,32,128,2048]{3,2,1,0:T(8,128)(2,1)} %bitcast.27, bf16[2,2,128,2048]{3,2,1,0:T(8,128)(2,1)} %collective-permute-done.9.refs_1_.refs_7_, bf16[2,2,16,128,2048]{4,3,2,1,0:T(8,128)(2,1)} %bitcast.28, ...), custom_call_target="tpu_custom_call" | custom-call | tf_op jit(solution)/shard_map/pallas_call | solution.py:164
  73.1 8.3 %collective-permute-done.8.refs_4_.refs_12_ = bf16[128,2048]{1,0:T(8,128)(2,1)} collective-permute-done((bf16[128,2048]{1,0:T(8,128)(2,1)}, bf16[128,2048]{1,0:T(8,128)(2,1)}, u32[]{:S(2)}, u32[]{:S(2)}) %collective-permute-start.8) | collective-permute-done | bytes 524320 | tf_op jit(solution)/shard_map/ppermute | solution.py:151
  95.3 6.3 %collective-permute-done.16.refs_6_.refs_12_ = bf16[128,2048]{1,0:T(8,128)(2,1)} collective-permute-done((bf16[128,2048]{1,0:T(8,128)(2,1)}, bf16[128,2048]{1,0:T(8,128)(2,1)}, u32[]{:S(2)}, u32[]{:S(2)}) %collective-permute-start.16) | collective-permute-done | bytes 524320 | tf_op jit(solution)/shard_map/ppermute | solution.py:151
  107.2 5.7 %collective-permute-done.19.refs_13_.refs_14_ = bf16[128,2048]{1,0:T(8,128)(2,1)} collective-permute-done((bf16[128,2048]{1,0:T(8,128)(2,1)}, bf16[128,2048]{1,0:T(8,128)(2,1)}, u32[]{:S(2)}, u32[]{:S(2)}) %collective-permute-start.19) | collective-permute-done | bytes 524320 | tf_op jit(solution)/shard_map/ppermute | solution.py:151
  112.9 6.7 %shard_map.55 = (bf16[128,2048]{1,0:T(8,128)(2,1)}, bf16[128,2048]{1,0:T(8,128)(2,1)}) custom-call(s32[4]{0:T(128)} %pad_add_fusion.place, bf16[2,32,128,2048]{3,2,1,0:T(8,128)(2,1)} %bitcast.33, bf16[2,2,128,2048]{3,2,1,0:T(8,128)(2,1)} %collective-permute-done.6.refs_1_.refs_7_, bf16[32,128,128]{2,1,0:T(8,128)(2,1)} %bitcast.7.refs_2_.refs_8_, ...), custom_call_target="tpu_custom_call" | custom-call | tf_op jit(solution)/shard_map/pallas_call | solution.py:164
  124.1 6.6 %shard_map.56 = (bf16[128,2048]{1,0:T(8,128)(2,1)}, bf16[128,2048]{1,0:T(8,128)(2,1)}) custom-call(s32[4]{0:T(128)} %pad_add_fusion.place, bf16[2,32,128,2048]{3,2,1,0:T(8,128)(2,1)} %bitcast.35, bf16[2,2,128,2048]{3,2,1,0:T(8,128)(2,1)} %collective-permute-done.9.refs_1_.refs_7_, bf16[32,128,128]{2,1,0:T(8,128)(2,1)} %bitcast.7.refs_2_.refs_8_, ...), custom_call_target="tpu_custom_call" | custom-call | tf_op jit(solution)/shard_map/pallas_call | solution.py:164
  139.1 6.8 %shard_map.57 = (bf16[128,2048]{1,0:T(8,128)(2,1)}, bf16[128,2048]{1,0:T(8,128)(2,1)}) custom-call(s32[4]{0:T(128)} %pad_add_fusion.place, bf16[2,32,128,2048]{3,2,1,0:T(8,128)(2,1)} %bitcast.37, bf16[2,2,128,2048]{3,2,1,0:T(8,128)(2,1)} %collective-permute-done.3.refs_1_.refs_7_, bf16[32,128,128]{2,1,0:T(8,128)(2,1)} %bitcast.7.refs_2_.refs_8_, ...), custom_call_target="tpu_custom_call" | custom-call | tf_op jit(solution)/shard_map/pallas_call | solution.py:164
  149.7 7.3 %shard_map.58 = (bf16[128,2048]{1,0:T(8,128)(2,1)}, bf16[128,2048]{1,0:T(8,128)(2,1)}, bf16[128,2048]{1,0:T(8,128)(2,1)}) custom-call(s32[4]{0:T(128)} %pad_add_fusion.place, bf16[2,32,128,2048]{3,2,1,0:T(8,128)(2,1)} %bitcast.39, bf16[2,2,128,2048]{3,2,1,0:T(8,128)(2,1)} %collective-permute-done.14.refs_1_.refs_7_, ...), custom_call_target="tpu_custom_call" | custom-call | tf_op jit(solution)/shard_map/pallas_call | solution.py:164
  159.2 19.8 %collective-permute-start.32 = (bf16[128,2048]{1,0:T(8,128)(2,1)}, bf16[128,2048]{1,0:T(8,128)(2,1)}, u32[]{:S(2)}, u32[]{:S(2)}) collective-permute-start(bf16[128,2048]{1,0:T(8,128)(2,1)} %get-tuple-element.57), channel_id=1, source_target_pairs={{0,5},{1,4},{2,7},{3,6},{4,1},{5,0},{6,3},{7,2},{8,13},{9,12},{10,... | collective-permute-start | bytes 1572872 | tf_op jit(solution)/shard_map/ppermute | solution.py:277
  179.0 7.2 %shard_map.59 = (bf16[128,2048]{1,0:T(8,128)(2,1)}, bf16[128,2048]{1,0:T(8,128)(2,1)}, bf16[128,2048]{1,0:T(8,128)(2,1)}) custom-call(s32[4]{0:T(128)} %pad_add_fusion.place, bf16[2,32,128,2048]{3,2,1,0:T(8,128)(2,1)} %bitcast.41, bf16[2,2,128,2048]{3,2,1,0:T(8,128)(2,1)} %collective-permute-done.25.refs_1_, bf16[32,128,128]{2,1,0:T(8,128)(2,1)} %bitcast.7.refs_2_.refs_8_, ...), custom_call_target="tpu_custom_call" | custom-call | tf_op jit(solution)/shard_map/pallas_call | solution.py:164
  188.4 12.3 %collective-permute-start.36 = (bf16[128,2048]{1,0:T(8,128)(2,1)}, bf16[128,2048]{1,0:T(8,128)(2,1)}, u32[]{:S(2)}, u32[]{:S(2)}) collective-permute-start(bf16[128,2048]{1,0:T(8,128)(2,1)} %get-tuple-element.60), channel_id=1, source_target_pairs={{0,4},{1,5},{2,6},{3,7},{4,0},{5,1},{6,2},{7,3},{8,12},{9,13},{10,... | collective-permute-start | bytes 1572872 | tf_op jit(solution)/shard_map/ppermute | solution.py:277
  200.6 7.2 %shard_map.60 = (bf16[128,2048]{1,0:T(8,128)(2,1)}, bf16[128,2048]{1,0:T(8,128)(2,1)}, bf16[128,2048]{1,0:T(8,128)(2,1)}) custom-call(s32[4]{0:T(128)} %pad_add_fusion.place, bf16[2,32,128,2048]{3,2,1,0:T(8,128)(2,1)} %bitcast.43, bf16[2,2,128,2048]{3,2,1,0:T(8,128)(2,1)} %collective-permute-done.11.refs_1_, bf16[32,128,128]{2,1,0:T(8,128)(2,1)} %bitcast.7.refs_2_.refs_8_, ...), custom_call_target="tpu_custom_call" | custom-call | tf_op jit(solution)/shard_map/pallas_call | solution.py:164
  207.8 11.1 %collective-permute-done.32 = bf16[128,2048]{1,0:T(8,128)(2,1)} collective-permute-done((bf16[128,2048]{1,0:T(8,128)(2,1)}, bf16[128,2048]{1,0:T(8,128)(2,1)}, u32[]{:S(2)}, u32[]{:S(2)}) %collective-permute-start.32) | collective-permute-done | bytes 524320 | tf_op jit(solution)/shard_map/ppermute | solution.py:277
  219.1 5.2 %shard_map.61.refs_5_ = bf16[128,2048]{1,0:T(8,128)(2,1)} custom-call(s32[4]{0:T(128)} %pad_add_fusion.place, bf16[2,32,128,2048]{3,2,1,0:T(8,128)(2,1)} %bitcast.45, bf16[2,2,128,2048]{3,2,1,0:T(8,128)(2,1)} %collective-permute-done.25.refs_1_, bf16[32,128,128]{2,1,0:T(8,128)(2,1)} %bitcast.7.refs_2_.refs_8_, bf16[32,128,128]{2,1,0:T(8,128)(2,1)} %bitcast.8.refs_3_.refs_9_, ...), custom_call_target="tpu_custom_call" | custom-call | tf_op jit(solution)/shard_map/pallas_call | solution.py:164
  229.7 6.0 %shard_map.62.refs_3_ = bf16[128,16384]{1,0:T(8,128)(2,1)} custom-call(s32[4]{0:T(128)} %pad_add_fusion.place, bf16[1,128,2048]{2,1,0:T(8,128)(2,1)} %bitcast.10.refs_15_.refs_0_, bf16[1,128,2048]{2,1,0:T(8,128)(2,1)} %bitcast.9.refs_16_.refs_1_, bf16[1,128,2048]{2,1,0:T(8,128)(2,1)} %bitcast.11.refs_10_.refs_2_, bf16[1,128,2048]{2,1,0:T(8,128)(2,1)} %bitcast.15.refs_3_, ...), custom_call_target="tpu_custom_call" | custom-call | tf_op jit(solution)/shard_map/pallas_call | solution.py:164
  235.7 5.1 %collective-permute-done.35 = bf16[128,2048]{1,0:T(8,128)(2,1)} collective-permute-done((bf16[128,2048]{1,0:T(8,128)(2,1)}, bf16[128,2048]{1,0:T(8,128)(2,1)}, u32[]{:S(2)}, u32[]{:S(2)}) %collective-permute-start.35) | collective-permute-done | bytes 524320 | tf_op jit(solution)/shard_map/ppermute | solution.py:277
  248.3 5.1 %shard_map.65 = bf16[128,16384]{1,0:T(8,128)(2,1)} custom-call(s32[4]{0:T(128)} %pad_add_fusion.place, bf16[2,32,128,2048]{3,2,1,0:T(8,128)(2,1)} %bitcast.46, bf16[2,2,128,2048]{3,2,1,0:T(8,128)(2,1)} %collective-permute-done.11.refs_1_, bf16[32,128,128]{2,1,0:T(8,128)(2,1)} %bitcast.7.refs_2_.refs_8_, ...), custom_call_target="tpu_custom_call", output_to_operand_aliasing={{}: (10, {})} | custom-call | tf_op jit(solution)/shard_map/pallas_call | solution.py:164
  (81 shorter events, 80.2 us)
Async XLA Ops:
  7.8 18.0 %collective-permute-start = (bf16[2,2,128,2048]{3,2,1,0:T(8,128)(2,1)}, bf16[2,2,128,2048]{3,2,1,0:T(8,128)(2,1)}, u32[]{:S(2)}, u32[]{:S(2)}) collective-permute-start(bf16[2,2,128,2048]{3,2,1,0:T(8,128)(2,1)} %get-tuple-element.33.refs_5_), channel_id=1, source_target_pairs={{0,8},{8,0},{16,24},{24,16},{1,9},{9,1},{17,25},{25,17},{2,10},{10... | collective-permute-start | bytes 6291464 | tf_op jit(solution)/shard_map/ppermute | solution.py:148
  8.3 49.1 %collective-permute-start.6 = (bf16[2,2,128,2048]{3,2,1,0:T(8,128)(2,1)}, bf16[2,2,128,2048]{3,2,1,0:T(8,128)(2,1)}, u32[]{:S(2)}, u32[]{:S(2)}) collective-permute-start(bf16[2,2,128,2048]{3,2,1,0:T(8,128)(2,1)} %get-tuple-element.36), channel_id=1, source_target_pairs={{0,8},{8,0},{16,24},{24,16},{1,9},{9,1},{17,25},{25,17},{2,10},{10... | collective-permute-start | bytes 6291464 | tf_op jit(solution)/shard_map/ppermute | solution.py:148
  25.8 42.4 %collective-permute-start.9 = (bf16[2,2,128,2048]{3,2,1,0:T(8,128)(2,1)}, bf16[2,2,128,2048]{3,2,1,0:T(8,128)(2,1)}, u32[]{:S(2)}, u32[]{:S(2)}) collective-permute-start(bf16[2,2,128,2048]{3,2,1,0:T(8,128)(2,1)} %get-tuple-element.39), channel_id=1, source_target_pairs={{0,8},{8,0},{16,24},{24,16},{1,9},{9,1},{17,25},{25,17},{2,10},{10... | collective-permute-start | bytes 6291464 | tf_op jit(solution)/shard_map/ppermute | solution.py:148
  30.0 51.4 %collective-permute-start.3 = (bf16[2,2,128,2048]{3,2,1,0:T(8,128)(2,1)}, bf16[2,2,128,2048]{3,2,1,0:T(8,128)(2,1)}, u32[]{:S(2)}, u32[]{:S(2)}) collective-permute-start(bf16[2,2,128,2048]{3,2,1,0:T(8,128)(2,1)} %get-tuple-element.35), channel_id=1, source_target_pairs={{0,8},{8,0},{16,24},{24,16},{1,9},{9,1},{17,25},{25,17},{2,10},{10... | collective-permute-start | bytes 6291464 | tf_op jit(solution)/shard_map/ppermute | solution.py:148
  57.4 28.6 %collective-permute-start.12 = (bf16[4096,128]{1,0:T(8,128)(2,1)}, bf16[4096,128]{1,0:T(8,128)(2,1)}, u32[]{:S(2)}, u32[]{:S(2)}) collective-permute-start(bf16[4096,128]{1,0:T(8,128)(2,1)} %pad_maximum_fusion.refs_3_), channel_id=1, source_target_pairs={{0,8},{8,0},{16,24},{24,16},{1,9},{9,1},{17,25},{25,17},{2,10},{10... | collective-permute-start | bytes 3145736 | tf_op jit(solution)/shard_map/ppermute | solution.py:148
  68.2 39.0 %collective-permute-start.18 = (bf16[2,1,128,2048]{3,2,1,0:T(8,128)(2,1)}, bf16[2,1,128,2048]{3,2,1,0:T(8,128)(2,1)}, u32[]{:S(2)}, u32[]{:S(2)}) collective-permute-start(bf16[2,1,128,2048]{3,2,1,0:T(8,128)(2,1)} %get-tuple-element.44), channel_id=1, source_target_pairs={{0,8},{8,0},{16,24},{24,16},{1,9},{9,1},{17,25},{25,17},{2,10},{10... | collective-permute-start | bytes 3145736 | tf_op jit(solution)/shard_map/ppermute | solution.py:148
  81.4 64.6 %collective-permute-start.14 = (bf16[2,2,128,2048]{3,2,1,0:T(8,128)(2,1)}, bf16[2,2,128,2048]{3,2,1,0:T(8,128)(2,1)}, u32[]{:S(2)}, u32[]{:S(2)}) collective-permute-start(bf16[2,2,128,2048]{3,2,1,0:T(8,128)(2,1)} %get-tuple-element.42), channel_id=1, source_target_pairs={{0,8},{8,0},{16,24},{24,16},{1,9},{9,1},{17,25},{25,17},{2,10},{10... | collective-permute-start | bytes 6291464 | tf_op jit(solution)/shard_map/ppermute | solution.py:148
  81.4 77.7 %collective-permute-start.25 = (bf16[2,2,128,2048]{3,2,1,0:T(8,128)(2,1)}, bf16[2,2,128,2048]{3,2,1,0:T(8,128)(2,1)}, u32[]{:S(2)}, u32[]{:S(2)}) collective-permute-start(bf16[2,2,128,2048]{3,2,1,0:T(8,128)(2,1)} %get-tuple-element.51), channel_id=1, source_target_pairs={{0,8},{8,0},{16,24},{24,16},{1,9},{9,1},{17,25},{25,17},{2,10},{10... | collective-permute-start | bytes 6291464 | tf_op jit(solution)/shard_map/ppermute | solution.py:148
  94.3 18.6 %collective-permute-start.19 = (bf16[128,2048]{1,0:T(8,128)(2,1)}, bf16[128,2048]{1,0:T(8,128)(2,1)}, u32[]{:S(2)}, u32[]{:S(2)}) collective-permute-start(bf16[128,2048]{1,0:T(8,128)(2,1)} %shard_map.53.refs_7_), channel_id=1, source_target_pairs={{0,16},{8,24},{16,0},{24,8},{1,17},{9,25},{17,1},{25,9},{2,18},{10... | collective-permute-start | bytes 1572872 | tf_op jit(solution)/shard_map/ppermute | solution.py:151
  105.6 18.6 %collective-permute-start.17 = (bf16[128,2048]{1,0:T(8,128)(2,1)}, bf16[128,2048]{1,0:T(8,128)(2,1)}, u32[]{:S(2)}, u32[]{:S(2)}) collective-permute-start(bf16[128,2048]{1,0:T(8,128)(2,1)} %shard_map.54.refs_15_), channel_id=1, source_target_pairs={{0,16},{8,24},{16,0},{24,8},{1,17},{9,25},{17,1},{25,9},{2,18},{10... | collective-permute-start | bytes 1572872 | tf_op jit(solution)/shard_map/ppermute | solution.py:151
  107.1 93.5 %collective-permute-start.11 = (bf16[2,2,128,2048]{3,2,1,0:T(8,128)(2,1)}, bf16[2,2,128,2048]{3,2,1,0:T(8,128)(2,1)}, u32[]{:S(2)}, u32[]{:S(2)}) collective-permute-start(bf16[2,2,128,2048]{3,2,1,0:T(8,128)(2,1)} %get-tuple-element.41), channel_id=1, source_target_pairs={{0,8},{8,0},{16,24},{24,16},{1,9},{9,1},{17,25},{25,17},{2,10},{10... | collective-permute-start | bytes 6291464 | tf_op jit(solution)/shard_map/ppermute | solution.py:148
  135.4 21.7 %collective-permute-start.27 = (bf16[128,2048]{1,0:T(8,128)(2,1)}, bf16[128,2048]{1,0:T(8,128)(2,1)}, u32[]{:S(2)}, u32[]{:S(2)}) collective-permute-start(bf16[128,2048]{1,0:T(8,128)(2,1)} %get-tuple-element.52), channel_id=1, source_target_pairs={{0,7},{1,6},{2,5},{3,4},{4,3},{5,2},{6,1},{7,0},{8,15},{9,14},{10,... | collective-permute-start | bytes 1572872 | tf_op jit(solution)/shard_map/ppermute | solution.py:277
  147.6 38.6 %collective-permute-start.24 = (bf16[128,2048]{1,0:T(8,128)(2,1)}, bf16[128,2048]{1,0:T(8,128)(2,1)}, u32[]{:S(2)}, u32[]{:S(2)}) collective-permute-start(bf16[128,2048]{1,0:T(8,128)(2,1)} %get-tuple-element.50), channel_id=1, source_target_pairs={{0,6},{1,7},{2,4},{3,5},{4,2},{5,3},{6,0},{7,1},{8,14},{9,15},{10,... | collective-permute-start | bytes 1572872 | tf_op jit(solution)/shard_map/ppermute | solution.py:277
  157.0 30.5 %collective-permute-start.23 = (bf16[128,2048]{1,0:T(8,128)(2,1)}, bf16[128,2048]{1,0:T(8,128)(2,1)}, u32[]{:S(2)}, u32[]{:S(2)}) collective-permute-start(bf16[128,2048]{1,0:T(8,128)(2,1)} %get-tuple-element.49), channel_id=1, source_target_pairs={{0,16},{8,24},{16,0},{24,8},{1,17},{9,25},{17,1},{25,9},{2,18},{10... | collective-permute-start | bytes 1572872 | tf_op jit(solution)/shard_map/ppermute | solution.py:151
  159.1 29.3 %collective-permute-start.22 = (bf16[128,2048]{1,0:T(8,128)(2,1)}, bf16[128,2048]{1,0:T(8,128)(2,1)}, u32[]{:S(2)}, u32[]{:S(2)}) collective-permute-start(bf16[128,2048]{1,0:T(8,128)(2,1)} %get-tuple-element.48.refs_16_), channel_id=1, source_target_pairs={{0,16},{8,24},{16,0},{24,8},{1,17},{9,25},{17,1},{25,9},{2,18},{10... | collective-permute-start | bytes 1572872 | tf_op jit(solution)/shard_map/ppermute | solution.py:151
  159.2 59.7 %collective-permute-start.32 = (bf16[128,2048]{1,0:T(8,128)(2,1)}, bf16[128,2048]{1,0:T(8,128)(2,1)}, u32[]{:S(2)}, u32[]{:S(2)}) collective-permute-start(bf16[128,2048]{1,0:T(8,128)(2,1)} %get-tuple-element.57), channel_id=1, source_target_pairs={{0,5},{1,4},{2,7},{3,6},{4,1},{5,0},{6,3},{7,2},{8,13},{9,12},{10,... | collective-permute-start | bytes 1572872 | tf_op jit(solution)/shard_map/ppermute | solution.py:277
  186.3 32.9 %collective-permute-start.31 = (bf16[128,2048]{1,0:T(8,128)(2,1)}, bf16[128,2048]{1,0:T(8,128)(2,1)}, u32[]{:S(2)}, u32[]{:S(2)}) collective-permute-start(bf16[128,2048]{1,0:T(8,128)(2,1)} %get-tuple-element.56), channel_id=1, source_target_pairs={{0,16},{8,24},{16,0},{24,8},{1,17},{9,25},{17,1},{25,9},{2,18},{10... | collective-permute-start | bytes 1572872 | tf_op jit(solution)/shard_map/ppermute | solution.py:151
  187.6 31.6 %collective-permute-start.30 = (bf16[128,2048]{1,0:T(8,128)(2,1)}, bf16[128,2048]{1,0:T(8,128)(2,1)}, u32[]{:S(2)}, u32[]{:S(2)}) collective-permute-start(bf16[128,2048]{1,0:T(8,128)(2,1)} %get-tuple-element.53.refs_17_), channel_id=1, source_target_pairs={{0,16},{8,24},{16,0},{24,8},{1,17},{9,25},{17,1},{25,9},{2,18},{10... | collective-permute-start | bytes 1572872 | tf_op jit(solution)/shard_map/ppermute | solution.py:151
  188.4 40.3 %collective-permute-start.36 = (bf16[128,2048]{1,0:T(8,128)(2,1)}, bf16[128,2048]{1,0:T(8,128)(2,1)}, u32[]{:S(2)}, u32[]{:S(2)}) collective-permute-start(bf16[128,2048]{1,0:T(8,128)(2,1)} %get-tuple-element.60), channel_id=1, source_target_pairs={{0,4},{1,5},{2,6},{3,7},{4,0},{5,1},{6,2},{7,3},{8,12},{9,13},{10,... | collective-permute-start | bytes 1572872 | tf_op jit(solution)/shard_map/ppermute | solution.py:277
  200.6 35.0 %collective-permute-start.34 = (bf16[128,2048]{1,0:T(8,128)(2,1)}, bf16[128,2048]{1,0:T(8,128)(2,1)}, u32[]{:S(2)}, u32[]{:S(2)}) collective-permute-start(bf16[128,2048]{1,0:T(8,128)(2,1)} %get-tuple-element.58), channel_id=1, source_target_pairs={{0,3},{1,2},{2,1},{3,0},{4,7},{5,6},{6,5},{7,4},{8,11},{9,10},{10,... | collective-permute-start | bytes 1572872 | tf_op jit(solution)/shard_map/ppermute | solution.py:277
  219.0 21.8 %collective-permute-start.35 = (bf16[128,2048]{1,0:T(8,128)(2,1)}, bf16[128,2048]{1,0:T(8,128)(2,1)}, u32[]{:S(2)}, u32[]{:S(2)}) collective-permute-start(bf16[128,2048]{1,0:T(8,128)(2,1)} %get-tuple-element.59), channel_id=1, source_target_pairs={{0,2},{1,3},{2,0},{3,1},{4,6},{5,7},{6,4},{7,5},{8,10},{9,11},{10,... | collective-permute-start | bytes 1572872 | tf_op jit(solution)/shard_map/ppermute | solution.py:277
  224.3 20.2 %collective-permute-start.33 = (bf16[128,2048]{1,0:T(8,128)(2,1)}, bf16[128,2048]{1,0:T(8,128)(2,1)}, u32[]{:S(2)}, u32[]{:S(2)}) collective-permute-start(bf16[128,2048]{1,0:T(8,128)(2,1)} %shard_map.61.refs_5_), channel_id=1, source_target_pairs={{0,1},{1,0},{2,3},{3,2},{4,5},{5,4},{6,7},{7,6},{8,9},{9,8},{10,11... | collective-permute-start | bytes 1572872 | tf_op jit(solution)/shard_map/ppermute | solution.py:277
  225.4 22.3 %collective-permute-start.29 = (bf16[128,2048]{1,0:T(8,128)(2,1)}, bf16[128,2048]{1,0:T(8,128)(2,1)}, u32[]{:S(2)}, u32[]{:S(2)}) collective-permute-start(bf16[128,2048]{1,0:T(8,128)(2,1)} %get-tuple-element.55), channel_id=1, source_target_pairs={{0,16},{8,24},{16,0},{24,8},{1,17},{9,25},{17,1},{25,9},{2,18},{10... | collective-permute-start | bytes 1572872 | tf_op jit(solution)/shard_map/ppermute | solution.py:151
  228.7 19.6 %collective-permute-start.28 = (bf16[128,2048]{1,0:T(8,128)(2,1)}, bf16[128,2048]{1,0:T(8,128)(2,1)}, u32[]{:S(2)}, u32[]{:S(2)}) collective-permute-start(bf16[128,2048]{1,0:T(8,128)(2,1)} %get-tuple-element.54.refs_11_), channel_id=1, source_target_pairs={{0,16},{8,24},{16,0},{24,8},{1,17},{9,25},{17,1},{25,9},{2,18},{10... | collective-permute-start | bytes 1572872 | tf_op jit(solution)/shard_map/ppermute | solution.py:151
  (16 other events, 194.5 us)

commit v2 on v1

v2 whole, which is shorter than its diff:
```python
import functools

import jax
import jax.numpy as jnp
from jax import lax
from jax.experimental import pallas as pl
from jax.experimental.pallas import tpu as pltpu
from jax.sharding import PartitionSpec as P

F32 = jnp.float32
BF16 = jnp.bfloat16
TINY = 2.0**-126
UP_WEIGHTED = 2.0**3
UP_RATIO = 2.0**7
WINDOW = 3
LAG = 3
VMEM = 64 * 1024 * 1024 - 128 * 1024


def encode_total(t):
    t = t * 0.5
    for _ in range(5):
        t = t * t
    return t.astype(BF16)


def decode_total(code):
    t = code.astype(F32)
    for _ in range(4):
        t = lax.rsqrt(t)
    return 2.0 * t * lax.rsqrt(t)


def encode_signed(v, up):
    v = v * up
    v2 = v * v
    v4 = v2 * v2
    return (v4 * v2 * (v * jnp.abs(v))).astype(BF16)


def decode_signed(code, up):
    code = code.astype(F32)
    a = lax.rsqrt(jnp.maximum(jnp.abs(code), TINY))
    d = lax.rsqrt(lax.rsqrt(a))
    return code * a * (d * d * d) * (1.0 / up)


def sum_totals(fishers):
    total = None
    for ref in fishers:
        for lang in range(ref.shape[0]):
            wide = ref[lang].astype(F32)
            total = wide if total is None else total + wide
    return total


def sum_weighted(fishers, lefts, rights):
    weighted = None
    for ref, left, right in zip(fishers, lefts, rights):
        rank = right.shape[1]
        for lang in range(ref.shape[0]):
            change = jnp.dot(left[:, lang * rank : (lang + 1) * rank], right[lang], preferred_element_type=F32)
            term = ref[lang].astype(F32) * change
            weighted = term if weighted is None else weighted + term
    return weighted


def sum_all(place, half, own, peer, *factors):
    if half is None:
        left_own, left_peer, right_own, right_peer, *rest = factors
        lefts = (left_own[...], left_peer[...])
    else:
        own_low, own_high, peer_low, peer_high, right_own, right_peer, *rest = factors
        high = half(place) == 1
        lefts = (jnp.where(high, own_high[...], own_low[...]), jnp.where(high, peer_high[...], peer_low[...]))
    totals, weighted = None, None
    for ref, left, right in zip((own, peer), lefts, (right_own, right_peer)):
        rank = right.shape[1]
        for lang in range(ref.shape[0]):
            change = jnp.dot(left[:, lang * rank : (lang + 1) * rank], right[lang], preferred_element_type=F32)
            wide = ref[lang].astype(F32)
            totals = wide if totals is None else totals + wide
            weighted = wide * change if weighted is None else weighted + wide * change
    return totals, weighted, rest


def copy_body(pieces, steps, place, src, out, held, into, outof):
    high, core, side = place[0], place[1], place[2]
    copies = []
    for i, (step, far) in enumerate(pieces):
        band = (1 - core) * steps + lax.bitwise_xor(high, step)
        for lang in range(src.shape[0]):
            rows = src.at[lang, 1 - side if far else side, band]
            first = pltpu.make_async_copy(rows, held.at[i, lang], into.at[i, lang])
            first.start()
            copies.append((first, pltpu.make_async_copy(held.at[i, lang], out.at[i, lang], outof.at[i, lang])))
    for first, second in copies:
        first.wait()
        second.start()
    for _, second in copies:
        second.wait()


def join_body(place, first, second, out):
    count = first.shape[0]
    out[:count] = first[...]
    out[count:] = second[...]


def totals_body(place, own, peer, out):
    out[...] = encode_total(sum_totals((own, peer)))


def many_totals_body(place, *refs):
    out = refs[-1]
    for i in range(out.shape[0]):
        out[i] = encode_total(sum_totals(refs[2 * i : 2 * i + 2]))


def weighted_body(half, place, *refs):
    _, weighted, (out,) = sum_all(place, half, *refs)
    out[...] = encode_signed(weighted, UP_WEIGHTED)


def ratio(half, place, *refs):
    totals, weighted, (total_code, weighted_code, *rest) = sum_all(place, half, *refs)
    return (weighted + decode_signed(weighted_code[...], UP_WEIGHTED)) / (totals + decode_total(total_code[...])), rest


def ratio_body(half, place, *refs):
    value, (out,) = ratio(half, place, *refs)
    out[...] = encode_signed(value, UP_RATIO)


def merge_own_body(half, place, *refs):
    value, (base, out) = ratio(half, place, *refs)
    out[...] = (base[...].astype(F32) + value).astype(BF16)


def merge_body(place, code, base, out):
    out[...] = (base[...].astype(F32) + decode_signed(code[...], UP_RATIO)).astype(BF16)


def merge_many_body(place, *refs):
    *codes, base, out = refs
    for i, code in enumerate(codes):

        @pl.when(pl.program_id(0) == i)
        def _():
            merge_body(place, code, base, out)


def run_parts(parts, skipped, scratch, place, *refs):
    taken = sum(count for _, count, _ in parts)
    ins, outs, own = refs[:taken], refs[taken + skipped : len(refs) - scratch], refs[len(refs) - scratch :]
    for body, count, results in parts:
        body(place, *ins[:count], *outs[:results], *own)
        ins, outs = ins[count:], outs[results:]


def shards(fisher, factor_left, factor_right, base_weight):
    lang_count = lax.axis_size("lang")
    blk_count = lax.axis_size("blk")
    langs, full_rows, cols = fisher.shape
    rows = base_weight.shape[0]
    rank = factor_right.shape[1]
    steps = 8
    group = blk_count // steps
    band = group * rows
    tile = min(1024, cols)
    tiles = cols // tile
    half = lang_count // 2
    sides = half

    lang, blk = lax.axis_index("lang"), lax.axis_index("blk")
    core, side = lax.rem(lang, 2), lax.div(lang, 2)
    high = lax.div(blk, group)

    def over_core(a):
        return lax.ppermute(a, "lang", [(i, i ^ 1) for i in range(lang_count)])

    def over_x(a):
        return lax.ppermute(a, "lang", [(i, i ^ half) for i in range(lang_count)])

    bands = fisher.reshape(langs, lang_count * steps, band, cols)
    by_owner = fisher.reshape(langs, sides, 2 * steps, band, cols)

    ANY = pl.BlockSpec(memory_space=pl.ANY)
    last = [None]

    def call(parts, deps=(), alias=None, grid=(tiles,), scratch=()):
        counts = [(body, len(operands), len(shapes)) for body, operands, _, shapes, _ in parts]
        operands, specs, shapes, out_specs = ([one for part in parts for one in part[k]] for k in range(1, 5))
        deps = list(deps) + ([last[0]] if last[0] is not None and last[0] is not alias else [])
        tail = deps + ([alias] if alias is not None else [])
        results = pl.pallas_call(
            functools.partial(run_parts, counts, len(tail), len(scratch)),
            out_shape=shapes,
            grid_spec=pltpu.PrefetchScalarGridSpec(
                num_scalar_prefetch=1,
                grid=grid,
                in_specs=specs + [ANY] * len(tail),
                out_specs=out_specs,
                scratch_shapes=list(scratch),
            ),
            input_output_aliases={} if alias is None else {len(operands) + len(tail): 0},
            compiler_params=pltpu.CompilerParams(vmem_limit_bytes=VMEM),
        )(place, *operands, *tail)
        last[0] = results[0]
        return list(results)

    place = jnp.stack([high, core, side, blk]).astype(jnp.int32)

    def owner(s, far, step):
        at_side = 1 - s[2] if far else s[2]
        return (at_side * 2 + s[1]) * steps + lax.bitwise_xor(s[0], step)

    right_peer = over_core(factor_right)
    left = factor_left.transpose(1, 0, 2).reshape(-1, langs * rank)
    shard_rows = left.shape[0]
    rounds = []
    relative = shard_rows % band == 0
    if relative:
        bit = blk_count // 2
        while bit:
            rounds.append(bit)
            bit //= 2
    else:
        left = lax.all_gather(left, "blk", axis=0, tiled=True)

    inside = max(shard_rows // band, 1)

    def apart(s, far, step):
        return lax.bitwise_xor(lax.div(owner(s, far, step), inside), s[3])

    def left_band(s, far, step):
        if not relative:
            return owner(s, far, step)
        rest, shard, bit = lax.div(apart(s, far, step), 2), 0, blk_count // 4
        while bit:
            shard, rest, bit = shard + lax.rem(rest, 2) * bit, lax.div(rest, 2), bit // 2
        return shard * inside + lax.rem(owner(s, far, step), inside)

    def which_half(far, step):
        if not relative:
            return None
        return lambda s: lax.rem(apart(s, far, step), 2)

    factors = []

    def has_left(parts):
        factors[:] = [part.reshape(-1, band, langs * rank) for part in (*parts, *map(over_core, parts))] + [factor_right, right_peer]

    if not relative:
        has_left([left])

    code_shape = jax.ShapeDtypeStruct((band, cols), BF16)
    out_shape = jax.ShapeDtypeStruct(base_weight.shape, BF16)

    right_spec = pl.BlockSpec((langs, rank, tile), lambda j, s: (0, 0, j))
    flat_spec = pl.BlockSpec((band, tile), lambda j, s: (0, j))

    def fisher_specs(far, step, piece):
        return (
            pl.BlockSpec((langs, None, band, tile), lambda j, s: (0, owner(s, far, step), 0, j)),
            pl.BlockSpec((None, langs, band, tile), lambda j, s: (piece, 0, 0, j)),
        )

    def factor_specs(far, step):
        return (
            *[pl.BlockSpec((None, band, langs * rank), lambda j, s: (left_band(s, far, step), 0, 0))] * (len(factors) - 2),
            right_spec,
            right_spec,
        )

    order = [7, 3, 6, 2, 5, 4, 1, 0]
    peers = {}
    arrived = {}
    crossed = []
    ratios = {}
    to_come = []

    def exchange(pieces, deps=()):
        count = len(pieces)
        scratch = [pltpu.VMEM((count, langs, band, cols), BF16)] + [pltpu.SemaphoreType.DMA((count, langs))] * 2
        shape = jax.ShapeDtypeStruct((count, langs, band, cols), BF16)
        out = call(
            [(functools.partial(copy_body, pieces, steps), (by_owner,), (ANY,), [shape], [ANY])],
            deps=deps,
            grid=(1,),
            scratch=scratch,
        )[0]
        out = over_core(out)
        for i, (step, far) in enumerate(pieces):
            peers[step, bool(far)] = (out, i)
        return out

    def send_part(body, step):
        peer, piece = peers[step, True]
        operands, specs = (bands, peer), fisher_specs(True, step, piece)
        if body is weighted_body:
            body = functools.partial(body, which_half(True, step))
            operands, specs = operands + tuple(factors), specs + factor_specs(True, step)
        return body, operands, specs, [code_shape], [flat_spec]

    def near_operands(step):
        peer, piece = peers[step, False]
        codes, specs = zip(*arrived[step])
        return (bands, peer, *factors, *codes), (*fisher_specs(False, step, piece), *factor_specs(False, step), *specs)

    def many_totals_part(those):
        operands, specs = [], []
        for step in those:
            peer, piece = peers[step, True]
            operands += [bands, peer]
            specs += fisher_specs(True, step, piece)
        shape = jax.ShapeDtypeStruct((len(those), band, cols), BF16)
        return many_totals_body, operands, specs, [shape], [pl.BlockSpec((len(those), band, tile), lambda j, s: (0, 0, j))]

    def divide_part(step):
        return functools.partial(ratio_body, which_half(False, step)), *near_operands(step), [code_shape], [flat_spec]

    def to_owner(step, code):
        if step:
            code = lax.ppermute(code, "blk", [(i, i ^ (step * group)) for i in range(blk_count)])
        if group > 1:
            near_groups = [[h * group + g for g in range(group)] for h in range(steps)]
            code = lax.all_to_all(code.reshape(group, rows, cols), "blk", 0, 0, axis_index_groups=near_groups, tiled=True)
        ratios[step] = code.reshape(group, rows, cols)

    def left_round():
        nonlocal left_from
        bit = rounds[joined]
        left_from = lax.ppermute(left, "blk", [(i, i ^ bit) for i in range(blk_count)])

    def join_part():
        count, width = left.shape
        half_spec = pl.BlockSpec((count, width), lambda j, s: (0, 0))
        whole_spec = pl.BlockSpec((2 * count, width), lambda j, s: (0, 0))
        return join_body, (left, left_from), (half_spec, half_spec), [jax.ShapeDtypeStruct((2 * count, width), BF16)], [whole_spec]

    left_from, joined = None, 0
    if relative:
        left_round()

    def stage(send=None, divide=None, deps=(), join=False):
        nonlocal left, joined
        join = join and relative
        parts = []
        if send is not None:
            parts.append(many_totals_part(send[1]) if isinstance(send[1], list) else send_part(*send))
        if divide is not None:
            parts.append(divide_part(divide))
        if join:
            parts.append(join_part())
        if not parts:
            return
        late = [code for at, code in to_come if at <= len(crossed) - LAG]
        to_come[:] = [(at, code) for at, code in to_come if at > len(crossed) - LAG]
        results = call(parts, deps=list(deps) + (crossed[-WINDOW:][:1] if len(crossed) >= WINDOW else []) + late)
        if send is not None:
            crossed.append(over_x(results.pop(0)))
            if isinstance(send[1], list):
                for i, step in enumerate(send[1]):
                    arrived[step] = [(crossed[-1], pl.BlockSpec((None, band, tile), lambda j, s, i=i: (i, 0, j)))]
            else:
                arrived.setdefault(send[1], []).append((crossed[-1], flat_spec))
        if divide is not None:
            to_owner(divide, results.pop(0))
            to_come.append((len(crossed) - 1, ratios[divide]))
        if join:
            left, joined = results.pop(0), joined + 1
            left_round()
            if joined == len(rounds) - 1:
                has_left([left, left_from])

    a = order
    first = exchange([(step, 1) for step in a[:4]])
    exchange([(step, 0) for step in a[:4]] + [(step, far) for step in a[4:] for far in (1, 0)], deps=[first, right_peer] + ([left_from] if relative else []))
    stage((totals_body, a[:4]), join=True)
    stage(join=True)
    stage((weighted_body, a[0]))
    stage((weighted_body, a[1]))
    stage((weighted_body, a[2]))
    stage((weighted_body, a[3]), divide=a[0])
    stage((totals_body, a[4]), divide=a[1])
    stage((weighted_body, a[4]), divide=a[2])
    stage((totals_body, a[5]), divide=a[3])
    stage((weighted_body, a[5]))
    stage((totals_body, a[6]), divide=a[4])
    stage((weighted_body, a[6]))
    stage((totals_body, a[7]), divide=a[5])
    stage((weighted_body, a[7]))
    stage(divide=a[6])
    merged = None

    def merge(done):
        nonlocal merged
        for part in range(group):

            def column(i, s, part=part):
                step = done[0]
                for n in range(1, len(done)):
                    step = jnp.where(i == n, done[n], step)
                return (0, lax.bitwise_xor(s[0], step) * group + part)

            code_spec = pl.BlockSpec((None, rows, cols), lambda i, s, part=part: (part, 0, 0))
            column_spec = pl.BlockSpec((rows, cols), column)
            merged = call(
                [(merge_many_body, (*(ratios[step] for step in done), base_weight), (code_spec,) * len(done) + (column_spec,), [out_shape], [column_spec])],
                alias=merged,
                grid=(len(done),),
            )[0]

    merge(a[:4])
    merge(a[4:6])
    if group == 1:
        merge(a[6:7])
        operands, specs = near_operands(a[7])
        column_spec = pl.BlockSpec((rows, tile), lambda j, s: (0, lax.bitwise_xor(s[0], a[7]) * tiles + j))
        merged = call([(functools.partial(merge_own_body, which_half(False, a[7])), (*operands, base_weight), (*specs, column_spec), [out_shape], [column_spec])], alias=merged)[0]
    else:
        stage(divide=a[7])
        merge(a[6:])
    return merged


def solution(mesh):
    placed = (
        P("lang", None, "blk"),
        P("lang", "blk", None),
        P("lang", None, "blk"),
        P(("lang", "blk"), None),
    )
    return jax.shard_map(
        shards, mesh=mesh, in_specs=placed, out_specs=P(("lang", "blk"), None), check_vma=False
    )
```

time: 254 us -> 236 us (0.929); the launches traced: 253 us -> 232 us
  starting transfers between devices: 69.1 us -> 43.1 us
  Pallas kernels: 101 us -> 110 us
  other arithmetic: 4.44 us -> 0.65 us
    ppermute x7, starting transfers between devices: 39.1 us -> 19.1 us  [to_owner(): lax.ppermute(code, 'blk', [(i, i ^ step * group) for i in range(blk_count)])]
    pallas_call x20 -> x21, Pallas kernels: 101 us -> 110 us  [call(): pl.pallas_call(functools.partial(run_parts, counts, len(tail), len(scratc...]
    ppermute x7, waiting for transfers between devices: 18.4 us -> 13.7 us  [to_owner(): lax.ppermute(code, 'blk', [(i, i ^ step * group) for i in range(blk_count)])]
    ppermute x16 -> x13, starting transfers between devices: 21.2 us -> 17.3 us  [over_x(): return lax.ppermute(a, 'lang', [(i, i ^ half) for i in range(lang_count)])]
    concatenate x3 -> x0, other arithmetic: 3.83 us -> none  [shards(): jnp.concatenate([left, lax.ppermute(left, 'blk', [(i, i ^ bit) for i in r...]
    ppermute x16 -> x13, waiting for transfers between devices: 33.6 us -> 32.3 us  [over_x(): return lax.ppermute(a, 'lang', [(i, i ^ half) for i in range(lang_count)])]
  transfers between devices with their start and end apart: 37 -> 28, of which waited for: 14 -> 13; matrix products, arithmetic and copies ran while one was open for 2% -> 0% of each run, Pallas kernels for 35% -> 39%
where the time goes in v2:
time: 236 us; the launch traced here: 232 us
  Pallas kernels  110 us (47%)
  waiting for transfers between devices  74.6 us (32%)
  starting transfers between devices  43.1 us (18%)
  local copies, waits for them, and re-layouts  3.29 us (1%)
    pallas_call x21, Pallas kernels, call(): pl.pallas_call(functools.partial(run_parts, counts, len(tail), len(scratc...  110 us
    ppermute x13, waiting for transfers between devices, over_x(): return lax.ppermute(a, 'lang', [(i, i ^ half) for i in range(lang_count)])  32.3 us
    ppermute x3, waiting for transfers between devices, left_round(): lax.ppermute(left, 'blk', [(i, i ^ bit) for i in range(blk_count)])  26.7 us
    ppermute x7, starting transfers between devices, to_owner(): lax.ppermute(code, 'blk', [(i, i ^ step * group) for i in range(blk_count)])  19.1 us
    ppermute x13, starting transfers between devices, over_x(): return lax.ppermute(a, 'lang', [(i, i ^ half) for i in range(lang_count)])  17.3 us
    ppermute x7, waiting for transfers between devices, to_owner(): lax.ppermute(code, 'blk', [(i, i ^ step * group) for i in range(blk_count)])  13.7 us
    ppermute x3, starting transfers between devices, left_round(): lax.ppermute(left, 'blk', [(i, i ^ bit) for i in range(blk_count)])  6.09 us
  transfers between devices with their start and end apart: 28, of which 13 were waited for; matrix products, arithmetic and copies ran while one was open for 0% of the time, Pallas kernels for 39%

profile of v2, /device:TPU:0, one launch (start us, length us, event | category | flops | bytes accessed | tf_op | source)
XLA Modules:
  0.0 231.8 jit_solution(16623722656749543299)
XLA Ops:
  0.7 4.2 %shard_map.46.refs_4_ = bf16[4,2,128,2048]{3,2,1,0:T(8,128)(2,1)} custom-call(s32[4]{0:T(128)} %pad_add_fusion.place, bf16[2,2,16,128,2048]{4,3,2,1,0:T(8,128)(2,1)} %bitcast.19), custom_call_target="tpu_custom_call" | custom-call | tf_op jit(solution)/shard_map/pallas_call | solution.py:196
  7.2 4.0 %collective-permute-start.2 = (bf16[512,128]{1,0:T(8,128)(2,1)S(1)}, bf16[512,128]{1,0:T(8,128)(2,1)}, u32[]{:S(2)}, u32[]{:S(2)}) collective-permute-start(bf16[512,128]{1,0:T(8,128)(2,1)S(1)} %copy.9.refs_8_), channel_id=1, source_target_pairs={{0,4},{1,5},{2,6},{3,7},{4,0},{5,1},{6,2},{7,3},{8,12},{9,13},{10,... | collective-permute-start | bytes 393224 | tf_op jit(solution)/shard_map/ppermute | solution.py:334
  11.2 6.7 %collective-permute-done.2.refs_3_.refs_9_ = bf16[512,128]{1,0:T(8,128)(2,1)} collective-permute-done((bf16[512,128]{1,0:T(8,128)(2,1)S(1)}, bf16[512,128]{1,0:T(8,128)(2,1)}, u32[]{:S(2)}, u32[]{:S(2)}) %collective-permute-start.2) | collective-permute-done | bytes 131104 | tf_op jit(solution)/shard_map/ppermute | solution.py:334
  17.9 10.2 %shard_map.47.refs_10_ = bf16[12,2,128,2048]{3,2,1,0:T(8,128)(2,1)} custom-call(s32[4]{0:T(128)} %pad_add_fusion.place, bf16[2,2,16,128,2048]{4,3,2,1,0:T(8,128)(2,1)} %bitcast.20, bf16[4,2,128,2048]{3,2,1,0:T(8,128)(2,1)} %collective-permute-done.refs_1_.refs_3_.refs_5_.refs_7_, ...), custom_call_target="tpu_custom_call" | custom-call | tf_op jit(solution)/shard_map/pallas_call | solution.py:196
  28.1 6.1 %shard_map.48 = (bf16[4,128,2048]{2,1,0:T(8,128)(2,1)}, bf16[1024,128]{1,0:T(8,128)(2,1)}) custom-call(s32[4]{0:T(128)} %pad_add_fusion.place, bf16[2,32,128,2048]{3,2,1,0:T(8,128)(2,1)} %bitcast.21, bf16[4,2,128,2048]{3,2,1,0:T(8,128)(2,1)} %collective-permute-done.refs_1_.refs_3_.refs_5_.refs_7_, bf16[2,32,128,2048]{3,2,1,0:T(8,128)(2,1)} %bitcast.22, ...), custom_call_target="tpu_custom_call" | custom-call | tf_op jit(solution)/shard_map/pallas_call | solution.py:196
  36.4 8.2 %collective-permute-done.4.refs_1_ = bf16[1024,128]{1,0:T(8,128)(2,1)} collective-permute-done((bf16[1024,128]{1,0:T(8,128)(2,1)}, bf16[1024,128]{1,0:T(8,128)(2,1)}, u32[]{:S(2)}, u32[]{:S(2)}) %collective-permute-start.4) | collective-permute-done | bytes 262176 | tf_op jit(solution)/shard_map/ppermute | solution.py:334
  48.7 11.9 %collective-permute-done.5 = bf16[2048,128]{1,0:T(8,128)(2,1)S(1)} collective-permute-done((bf16[2048,128]{1,0:T(8,128)(2,1)}, bf16[2048,128]{1,0:T(8,128)(2,1)S(1)}, u32[]{:S(2)}, u32[]{:S(2)}) %collective-permute-start.5) | collective-permute-done | bytes 524320 | tf_op jit(solution)/shard_map/ppermute | solution.py:334
  74.1 9.0 %collective-permute-done.8.refs_8_.refs_16_.refs_10_ = bf16[4,128,2048]{2,1,0:T(8,128)(2,1)} collective-permute-done((bf16[4,128,2048]{2,1,0:T(8,128)(2,1)}, bf16[4,128,2048]{2,1,0:T(8,128)(2,1)}, u32[]{:S(2)}, u32[]{:S(2)}) %collective-permute-start.8) | collective-permute-done | bytes 2097184 | tf_op jit(solution)/shard_map/ppermute | solution.py:183
  88.5 5.7 %collective-permute-done.9.refs_17_.refs_18_ = bf16[128,2048]{1,0:T(8,128)(2,1)} collective-permute-done((bf16[128,2048]{1,0:T(8,128)(2,1)}, bf16[128,2048]{1,0:T(8,128)(2,1)}, u32[]{:S(2)}, u32[]{:S(2)}) %collective-permute-start.9) | collective-permute-done | bytes 524320 | tf_op jit(solution)/shard_map/ppermute | solution.py:183
  94.3 7.0 %shard_map.53 = (bf16[128,2048]{1,0:T(8,128)(2,1)}, bf16[128,2048]{1,0:T(8,128)(2,1)}) custom-call(s32[4]{0:T(128)} %pad_add_fusion.place, bf16[2,32,128,2048]{3,2,1,0:T(8,128)(2,1)} %bitcast.28, bf16[4,2,128,2048]{3,2,1,0:T(8,128)(2,1)} %collective-permute-done.refs_1_.refs_3_.refs_5_.refs_7_, bf16[16,128,128]{2,1,0:T(8,128)(2,1)} %bitcast.48, ...), custom_call_target="tpu_custom_call" | custom-call | tf_op jit(solution)/shard_map/pallas_call | solution.py:196
  102.8 4.5 %collective-permute-start.11 = (bf16[128,2048]{1,0:T(8,128)(2,1)}, bf16[128,2048]{1,0:T(8,128)(2,1)}, u32[]{:S(2)}, u32[]{:S(2)}) collective-permute-start(bf16[128,2048]{1,0:T(8,128)(2,1)} %get-tuple-element.22), channel_id=1, source_target_pairs={{0,7},{1,6},{2,5},{3,4},{4,3},{5,2},{6,1},{7,0},{8,15},{9,14},{10,... | collective-permute-start | bytes 1572872 | tf_op jit(solution)/shard_map/ppermute | solution.py:325
  107.2 6.4 %shard_map.54 = (bf16[128,2048]{1,0:T(8,128)(2,1)}, bf16[128,2048]{1,0:T(8,128)(2,1)}) custom-call(s32[4]{0:T(128)} %pad_add_fusion.place, bf16[2,32,128,2048]{3,2,1,0:T(8,128)(2,1)} %bitcast.31, bf16[12,2,128,2048]{3,2,1,0:T(8,128)(2,1)} %collective-permute-done.3.refs_9_.refs_1_.refs_3_, bf16[2,32,128,2048]{3,2,1,0:T(8,128)(2,1)} %bitcast.30, ...), custom_call_target="tpu_custom_call" | custom-call | tf_op jit(solution)/shard_map/pallas_call | solution.py:196
  116.7 7.1 %shard_map.55 = (bf16[128,2048]{1,0:T(8,128)(2,1)}, bf16[128,2048]{1,0:T(8,128)(2,1)}) custom-call(s32[4]{0:T(128)} %pad_add_fusion.place, bf16[2,32,128,2048]{3,2,1,0:T(8,128)(2,1)} %bitcast.32, bf16[12,2,128,2048]{3,2,1,0:T(8,128)(2,1)} %collective-permute-done.3.refs_9_.refs_1_.refs_3_, bf16[16,128,128]{2,1,0:T(8,128)(2,1)} %bitcast.51, ...), custom_call_target="tpu_custom_call" | custom-call | tf_op jit(solution)/shard_map/pallas_call | solution.py:196
  131.5 6.4 %shard_map.56 = (bf16[128,2048]{1,0:T(8,128)(2,1)}, bf16[128,2048]{1,0:T(8,128)(2,1)}) custom-call(s32[4]{0:T(128)} %pad_add_fusion.place, bf16[2,32,128,2048]{3,2,1,0:T(8,128)(2,1)} %bitcast.34, bf16[12,2,128,2048]{3,2,1,0:T(8,128)(2,1)} %collective-permute-done.3.refs_9_.refs_1_.refs_3_, bf16[2,32,128,2048]{3,2,1,0:T(8,128)(2,1)} %bitcast.35, ...), custom_call_target="tpu_custom_call" | custom-call | tf_op jit(solution)/shard_map/pallas_call | solution.py:196
  139.4 4.3 %collective-permute-start.18 = (bf16[128,2048]{1,0:T(8,128)(2,1)}, bf16[128,2048]{1,0:T(8,128)(2,1)}, u32[]{:S(2)}, u32[]{:S(2)}) collective-permute-start(bf16[128,2048]{1,0:T(8,128)(2,1)} %get-tuple-element.27), channel_id=1, source_target_pairs={{0,2},{1,3},{2,0},{3,1},{4,6},{5,7},{6,4},{7,5},{8,10},{9,11},{10,... | collective-permute-start | bytes 1572872 | tf_op jit(solution)/shard_map/ppermute | solution.py:325
  150.4 6.4 %shard_map.58 = (bf16[128,2048]{1,0:T(8,128)(2,1)}, bf16[128,2048]{1,0:T(8,128)(2,1)}) custom-call(s32[4]{0:T(128)} %pad_add_fusion.place, bf16[2,32,128,2048]{3,2,1,0:T(8,128)(2,1)} %bitcast.37, bf16[12,2,128,2048]{3,2,1,0:T(8,128)(2,1)} %collective-permute-done.3.refs_9_.refs_1_.refs_3_, bf16[2,32,128,2048]{3,2,1,0:T(8,128)(2,1)} %bitcast.38, ...), custom_call_target="tpu_custom_call" | custom-call | tf_op jit(solution)/shard_map/pallas_call | solution.py:196
  158.5 4.2 %collective-permute-start.23 = (bf16[128,2048]{1,0:T(8,128)(2,1)}, bf16[128,2048]{1,0:T(8,128)(2,1)}, u32[]{:S(2)}, u32[]{:S(2)}) collective-permute-start(bf16[128,2048]{1,0:T(8,128)(2,1)} %get-tuple-element.31), channel_id=1, source_target_pairs={{0,5},{1,4},{2,7},{3,6},{4,1},{5,0},{6,3},{7,2},{8,13},{9,12},{10,... | collective-permute-start | bytes 1572872 | tf_op jit(solution)/shard_map/ppermute | solution.py:325
  168.1 4.8 %collective-permute-done.17.refs_11_.refs_12_ = bf16[128,2048]{1,0:T(8,128)(2,1)} collective-permute-done((bf16[128,2048]{1,0:T(8,128)(2,1)}, bf16[128,2048]{1,0:T(8,128)(2,1)}, u32[]{:S(2)}, u32[]{:S(2)}) %collective-permute-start.17) | collective-permute-done | bytes 524320 | tf_op jit(solution)/shard_map/ppermute | solution.py:183
  172.9 6.3 %shard_map.60 = (bf16[128,2048]{1,0:T(8,128)(2,1)}, bf16[128,2048]{1,0:T(8,128)(2,1)}) custom-call(s32[4]{0:T(128)} %pad_add_fusion.place, bf16[2,32,128,2048]{3,2,1,0:T(8,128)(2,1)} %bitcast.40, bf16[12,2,128,2048]{3,2,1,0:T(8,128)(2,1)} %collective-permute-done.3.refs_9_.refs_1_.refs_3_, bf16[2,32,128,2048]{3,2,1,0:T(8,128)(2,1)} %bitcast.41, ...), custom_call_target="tpu_custom_call" | custom-call | tf_op jit(solution)/shard_map/pallas_call | solution.py:196
  179.3 4.8 %collective-permute-done.22.refs_8_ = bf16[128,2048]{1,0:T(8,128)(2,1)} collective-permute-done((bf16[128,2048]{1,0:T(8,128)(2,1)}, bf16[128,2048]{1,0:T(8,128)(2,1)}, u32[]{:S(2)}, u32[]{:S(2)}) %collective-permute-start.22) | collective-permute-done | bytes 524320 | tf_op jit(solution)/shard_map/ppermute | solution.py:183
  184.1 13.7 %collective-permute-done.23 = bf16[128,2048]{1,0:T(8,128)(2,1)} collective-permute-done((bf16[128,2048]{1,0:T(8,128)(2,1)}, bf16[128,2048]{1,0:T(8,128)(2,1)}, u32[]{:S(2)}, u32[]{:S(2)}) %collective-permute-start.23) | collective-permute-done | bytes 524320 | tf_op jit(solution)/shard_map/ppermute | solution.py:325
  201.8 5.3 %shard_map.62.refs_5_ = bf16[128,2048]{1,0:T(8,128)(2,1)} custom-call(s32[4]{0:T(128)} %pad_add_fusion.place, bf16[2,32,128,2048]{3,2,1,0:T(8,128)(2,1)} %bitcast.43, bf16[12,2,128,2048]{3,2,1,0:T(8,128)(2,1)} %collective-permute-done.3.refs_9_.refs_1_.refs_3_, bf16[16,128,128]{2,1,0:T(8,128)(2,1)} %bitcast.59, bf16[16,128,128]{2,1,0:T(8,128)(2,1)} %bitcast.75, ...), custom_call_target="tpu_custom_call" | custom-call | tf_op jit(solution)/shard_map/pallas_call | solution.py:196
  210.7 6.0 %shard_map.63.refs_3_ = bf16[128,16384]{1,0:T(8,128)(2,1)} custom-call(s32[4]{0:T(128)} %pad_add_fusion.place, bf16[1,128,2048]{2,1,0:T(8,128)(2,1)} %bitcast.11.refs_13_.refs_0_, bf16[1,128,2048]{2,1,0:T(8,128)(2,1)} %bitcast.12.refs_9_.refs_1_, bf16[1,128,2048]{2,1,0:T(8,128)(2,1)} %bitcast.14.refs_13_.refs_2_, ...), custom_call_target="tpu_custom_call" | custom-call | tf_op jit(solution)/shard_map/pallas_call | solution.py:196
  226.6 5.2 %shard_map.66 = bf16[128,16384]{1,0:T(8,128)(2,1)} custom-call(s32[4]{0:T(128)} %pad_add_fusion.place, bf16[2,32,128,2048]{3,2,1,0:T(8,128)(2,1)} %bitcast.44, bf16[12,2,128,2048]{3,2,1,0:T(8,128)(2,1)} %collective-permute-done.3.refs_9_.refs_1_.refs_3_, bf16[16,128,128]{2,1,0:T(8,128)(2,1)} %bitcast.60, ...), custom_call_target="tpu_custom_call", output_to_operand_aliasing={{}: (12, {})} | custom-call | tf_op jit(solution)/shard_map/pallas_call | solution.py:196
  (63 shorter events, 73.4 us)
Async XLA Ops:
  4.9 13.0 %collective-permute-start = (bf16[4,2,128,2048]{3,2,1,0:T(8,128)(2,1)}, bf16[4,2,128,2048]{3,2,1,0:T(8,128)(2,1)}, u32[]{:S(2)}, u32[]{:S(2)}) collective-permute-start(bf16[4,2,128,2048]{3,2,1,0:T(8,128)(2,1)} %shard_map.46.refs_4_), channel_id=1, source_target_pairs={{0,8},{8,0},{16,24},{24,16},{1,9},{9,1},{17,25},{25,17},{2,10},{10... | collective-permute-start | bytes 12582920 | tf_op jit(solution)/shard_map/ppermute | solution.py:180
  28.0 66.2 %collective-permute-start.3 = (bf16[12,2,128,2048]{3,2,1,0:T(8,128)(2,1)}, bf16[12,2,128,2048]{3,2,1,0:T(8,128)(2,1)}, u32[]{:S(2)}, u32[]{:S(2)}) collective-permute-start(bf16[12,2,128,2048]{3,2,1,0:T(8,128)(2,1)} %shard_map.47.refs_10_), channel_id=1, source_target_pairs={{0,8},{8,0},{16,24},{24,16},{1,9},{9,1},{17,25},{25,17},{2,10},{10... | collective-permute-start | bytes 37748744 | tf_op jit(solution)/shard_map/ppermute | solution.py:180
  34.3 48.7 %collective-permute-start.8 = (bf16[4,128,2048]{2,1,0:T(8,128)(2,1)}, bf16[4,128,2048]{2,1,0:T(8,128)(2,1)}, u32[]{:S(2)}, u32[]{:S(2)}) collective-permute-start(bf16[4,128,2048]{2,1,0:T(8,128)(2,1)} %get-tuple-element.20.refs_2_), channel_id=1, source_target_pairs={{0,16},{8,24},{16,0},{24,8},{1,17},{9,25},{17,1},{25,9},{2,18},{10... | collective-permute-start | bytes 6291464 | tf_op jit(solution)/shard_map/ppermute | solution.py:183
  47.1 13.4 %collective-permute-start.5 = (bf16[2048,128]{1,0:T(8,128)(2,1)}, bf16[2048,128]{1,0:T(8,128)(2,1)S(1)}, u32[]{:S(2)}, u32[]{:S(2)}) collective-permute-start(bf16[2048,128]{1,0:T(8,128)(2,1)} %shard_map.49.refs_8_), channel_id=1, source_target_pairs={{0,1},{1,0},{2,3},{3,2},{4,5},{5,4},{6,7},{7,6},{8,9},{9,8},{10,11... | collective-permute-start | bytes 1572872 | tf_op jit(solution)/shard_map/ppermute | solution.py:334
  48.6 12.7 %collective-permute-start.6 = (bf16[2048,128]{1,0:T(8,128)(2,1)}, bf16[2048,128]{1,0:T(8,128)(2,1)S(1)}, u32[]{:S(2)}, u32[]{:S(2)}) collective-permute-start(bf16[2048,128]{1,0:T(8,128)(2,1)} %shard_map.49.refs_8_), channel_id=1, source_target_pairs={{0,8},{8,0},{16,24},{24,16},{1,9},{9,1},{17,25},{25,17},{2,10},{10... | collective-permute-start | bytes 1572872 | tf_op jit(solution)/shard_map/ppermute | solution.py:180
  68.0 26.2 %collective-permute-start.9 = (bf16[128,2048]{1,0:T(8,128)(2,1)}, bf16[128,2048]{1,0:T(8,128)(2,1)}, u32[]{:S(2)}, u32[]{:S(2)}) collective-permute-start(bf16[128,2048]{1,0:T(8,128)(2,1)} %shard_map.50.refs_8_), channel_id=1, source_target_pairs={{0,16},{8,24},{16,0},{24,8},{1,17},{9,25},{17,1},{25,9},{2,18},{10... | collective-permute-start | bytes 1572872 | tf_op jit(solution)/shard_map/ppermute | solution.py:183
  72.5 34.7 %collective-permute-start.13 = (bf16[128,2048]{1,0:T(8,128)(2,1)}, bf16[128,2048]{1,0:T(8,128)(2,1)}, u32[]{:S(2)}, u32[]{:S(2)}) collective-permute-start(bf16[128,2048]{1,0:T(8,128)(2,1)} %shard_map.51.refs_9_), channel_id=1, source_target_pairs={{0,16},{8,24},{16,0},{24,8},{1,17},{9,25},{17,1},{25,9},{2,18},{10... | collective-permute-start | bytes 1572872 | tf_op jit(solution)/shard_map/ppermute | solution.py:183
  87.0 29.7 %collective-permute-start.12 = (bf16[128,2048]{1,0:T(8,128)(2,1)}, bf16[128,2048]{1,0:T(8,128)(2,1)}, u32[]{:S(2)}, u32[]{:S(2)}) collective-permute-start(bf16[128,2048]{1,0:T(8,128)(2,1)} %shard_map.52.refs_19_), channel_id=1, source_target_pairs={{0,16},{8,24},{16,0},{24,8},{1,17},{9,25},{17,1},{25,9},{2,18},{10... | collective-permute-start | bytes 1572872 | tf_op jit(solution)/shard_map/ppermute | solution.py:183
  101.2 26.7 %collective-permute-start.10 = (bf16[128,2048]{1,0:T(8,128)(2,1)}, bf16[128,2048]{1,0:T(8,128)(2,1)}, u32[]{:S(2)}, u32[]{:S(2)}) collective-permute-start(bf16[128,2048]{1,0:T(8,128)(2,1)} %get-tuple-element.21.refs_13_), channel_id=1, source_target_pairs={{0,16},{8,24},{16,0},{24,8},{1,17},{9,25},{17,1},{25,9},{2,18},{10... | collective-permute-start | bytes 1572872 | tf_op jit(solution)/shard_map/ppermute | solution.py:183
  102.8 28.7 %collective-permute-start.11 = (bf16[128,2048]{1,0:T(8,128)(2,1)}, bf16[128,2048]{1,0:T(8,128)(2,1)}, u32[]{:S(2)}, u32[]{:S(2)}) collective-permute-start(bf16[128,2048]{1,0:T(8,128)(2,1)} %get-tuple-element.22), channel_id=1, source_target_pairs={{0,7},{1,6},{2,5},{3,4},{4,3},{5,2},{6,1},{7,0},{8,15},{9,14},{10,... | collective-permute-start | bytes 1572872 | tf_op jit(solution)/shard_map/ppermute | solution.py:325
  113.6 25.8 %collective-permute-start.15 = (bf16[128,2048]{1,0:T(8,128)(2,1)}, bf16[128,2048]{1,0:T(8,128)(2,1)}, u32[]{:S(2)}, u32[]{:S(2)}) collective-permute-start(bf16[128,2048]{1,0:T(8,128)(2,1)} %get-tuple-element.23.refs_19_), channel_id=1, source_target_pairs={{0,16},{8,24},{16,0},{24,8},{1,17},{9,25},{17,1},{25,9},{2,18},{10... | collective-permute-start | bytes 1572872 | tf_op jit(solution)/shard_map/ppermute | solution.py:183
  114.1 29.5 %collective-permute-start.16 = (bf16[128,2048]{1,0:T(8,128)(2,1)}, bf16[128,2048]{1,0:T(8,128)(2,1)}, u32[]{:S(2)}, u32[]{:S(2)}) collective-permute-start(bf16[128,2048]{1,0:T(8,128)(2,1)} %get-tuple-element.26), channel_id=1, source_target_pairs={{0,3},{1,2},{2,1},{3,0},{4,7},{5,6},{6,5},{7,4},{8,11},{9,10},{10,... | collective-permute-start | bytes 1572872 | tf_op jit(solution)/shard_map/ppermute | solution.py:325
  123.8 26.6 %collective-permute-start.19 = (bf16[128,2048]{1,0:T(8,128)(2,1)}, bf16[128,2048]{1,0:T(8,128)(2,1)}, u32[]{:S(2)}, u32[]{:S(2)}) collective-permute-start(bf16[128,2048]{1,0:T(8,128)(2,1)} %get-tuple-element.24.refs_14_), channel_id=1, source_target_pairs={{0,16},{8,24},{16,0},{24,8},{1,17},{9,25},{17,1},{25,9},{2,18},{10... | collective-permute-start | bytes 1572872 | tf_op jit(solution)/shard_map/ppermute | solution.py:183
  128.0 22.5 %collective-permute-start.20 = (bf16[128,2048]{1,0:T(8,128)(2,1)}, bf16[128,2048]{1,0:T(8,128)(2,1)}, u32[]{:S(2)}, u32[]{:S(2)}) collective-permute-start(bf16[128,2048]{1,0:T(8,128)(2,1)} %get-tuple-element.28), channel_id=1, source_target_pairs={{0,6},{1,7},{2,4},{3,5},{4,2},{5,3},{6,0},{7,1},{8,14},{9,15},{10,... | collective-permute-start | bytes 1572872 | tf_op jit(solution)/shard_map/ppermute | solution.py:325
  137.9 24.8 %collective-permute-start.14 = (bf16[128,2048]{1,0:T(8,128)(2,1)}, bf16[128,2048]{1,0:T(8,128)(2,1)}, u32[]{:S(2)}, u32[]{:S(2)}) collective-permute-start(bf16[128,2048]{1,0:T(8,128)(2,1)} %get-tuple-element.25.refs_10_), channel_id=1, source_target_pairs={{0,16},{8,24},{16,0},{24,8},{1,17},{9,25},{17,1},{25,9},{2,18},{10... | collective-permute-start | bytes 1572872 | tf_op jit(solution)/shard_map/ppermute | solution.py:183
  139.4 23.3 %collective-permute-start.18 = (bf16[128,2048]{1,0:T(8,128)(2,1)}, bf16[128,2048]{1,0:T(8,128)(2,1)}, u32[]{:S(2)}, u32[]{:S(2)}) collective-permute-start(bf16[128,2048]{1,0:T(8,128)(2,1)} %get-tuple-element.27), channel_id=1, source_target_pairs={{0,2},{1,3},{2,0},{3,1},{4,6},{5,7},{6,4},{7,5},{8,10},{9,11},{10,... | collective-permute-start | bytes 1572872 | tf_op jit(solution)/shard_map/ppermute | solution.py:325
  147.6 25.3 %collective-permute-start.17 = (bf16[128,2048]{1,0:T(8,128)(2,1)}, bf16[128,2048]{1,0:T(8,128)(2,1)}, u32[]{:S(2)}, u32[]{:S(2)}) collective-permute-start(bf16[128,2048]{1,0:T(8,128)(2,1)} %shard_map.57.refs_14_), channel_id=1, source_target_pairs={{0,16},{8,24},{16,0},{24,8},{1,17},{9,25},{17,1},{25,9},{2,18},{10... | collective-permute-start | bytes 1572872 | tf_op jit(solution)/shard_map/ppermute | solution.py:183
  156.8 27.3 %collective-permute-start.22 = (bf16[128,2048]{1,0:T(8,128)(2,1)}, bf16[128,2048]{1,0:T(8,128)(2,1)}, u32[]{:S(2)}, u32[]{:S(2)}) collective-permute-start(bf16[128,2048]{1,0:T(8,128)(2,1)} %get-tuple-element.29.refs_10_), channel_id=1, source_target_pairs={{0,16},{8,24},{16,0},{24,8},{1,17},{9,25},{17,1},{25,9},{2,18},{10... | collective-permute-start | bytes 1572872 | tf_op jit(solution)/shard_map/ppermute | solution.py:183
  158.5 39.4 %collective-permute-start.23 = (bf16[128,2048]{1,0:T(8,128)(2,1)}, bf16[128,2048]{1,0:T(8,128)(2,1)}, u32[]{:S(2)}, u32[]{:S(2)}) collective-permute-start(bf16[128,2048]{1,0:T(8,128)(2,1)} %get-tuple-element.31), channel_id=1, source_target_pairs={{0,5},{1,4},{2,7},{3,6},{4,1},{5,0},{6,3},{7,2},{8,13},{9,12},{10,... | collective-permute-start | bytes 1572872 | tf_op jit(solution)/shard_map/ppermute | solution.py:325
  166.7 35.1 %collective-permute-start.25 = (bf16[128,2048]{1,0:T(8,128)(2,1)}, bf16[128,2048]{1,0:T(8,128)(2,1)}, u32[]{:S(2)}, u32[]{:S(2)}) collective-permute-start(bf16[128,2048]{1,0:T(8,128)(2,1)} %shard_map.59.refs_13_), channel_id=1, source_target_pairs={{0,16},{8,24},{16,0},{24,8},{1,17},{9,25},{17,1},{25,9},{2,18},{10... | collective-permute-start | bytes 1572872 | tf_op jit(solution)/shard_map/ppermute | solution.py:183
  179.2 37.5 %collective-permute-start.27 = (bf16[128,2048]{1,0:T(8,128)(2,1)}, bf16[128,2048]{1,0:T(8,128)(2,1)}, u32[]{:S(2)}, u32[]{:S(2)}) collective-permute-start(bf16[128,2048]{1,0:T(8,128)(2,1)} %get-tuple-element.32), channel_id=1, source_target_pairs={{0,4},{1,5},{2,6},{3,7},{4,0},{5,1},{6,2},{7,3},{8,12},{9,13},{10,... | collective-permute-start | bytes 1572872 | tf_op jit(solution)/shard_map/ppermute | solution.py:325
  207.1 13.5 %collective-permute-start.26 = (bf16[128,2048]{1,0:T(8,128)(2,1)}, bf16[128,2048]{1,0:T(8,128)(2,1)}, u32[]{:S(2)}, u32[]{:S(2)}) collective-permute-start(bf16[128,2048]{1,0:T(8,128)(2,1)} %shard_map.62.refs_5_), channel_id=1, source_target_pairs={{0,1},{1,0},{2,3},{3,2},{4,5},{5,4},{6,7},{7,6},{8,9},{9,8},{10,11... | collective-permute-start | bytes 1572872 | tf_op jit(solution)/shard_map/ppermute | solution.py:325
  208.7 15.1 %collective-permute-start.21 = (bf16[128,2048]{1,0:T(8,128)(2,1)}, bf16[128,2048]{1,0:T(8,128)(2,1)}, u32[]{:S(2)}, u32[]{:S(2)}) collective-permute-start(bf16[128,2048]{1,0:T(8,128)(2,1)} %get-tuple-element.30.refs_10_), channel_id=1, source_target_pairs={{0,16},{8,24},{16,0},{24,8},{1,17},{9,25},{17,1},{25,9},{2,18},{10... | collective-permute-start | bytes 1572872 | tf_op jit(solution)/shard_map/ppermute | solution.py:183
  208.7 17.9 %collective-permute-start.24 = (bf16[128,2048]{1,0:T(8,128)(2,1)}, bf16[128,2048]{1,0:T(8,128)(2,1)}, u32[]{:S(2)}, u32[]{:S(2)}) collective-permute-start(bf16[128,2048]{1,0:T(8,128)(2,1)} %shard_map.61.refs_11_), channel_id=1, source_target_pairs={{0,16},{8,24},{16,0},{24,8},{1,17},{9,25},{17,1},{25,9},{2,18},{10... | collective-permute-start | bytes 1572872 | tf_op jit(solution)/shard_map/ppermute | solution.py:183
  (8 other events, 37.9 us)
